TPU v7x, 512 devices: a whole 4x8x8 slice. The times are simulated.
512 devices in a mesh: section: 16 (over z, core), tm: 32 (over x, y).
Axes of the slice: x: 4, y: 8, z: 8, core: 2. Of those that a mesh axis runs over, the one named last changes fastest.
Arguments:
- acts_in: bfloat16 [16, 4096, 2048], P('section', 'tm'), may hold values from -6 to 6
- saved_in: bfloat16 [16, 4096, 2048], P('section', 'tm'), may hold values from -6 to 6
- grad_in: bfloat16 [16, 4096, 2048], P('section', 'tm'), may hold values from -6 to 6
- gate_a: bfloat16 [16, 2, 8, 256, 256], P('section', None, None, 'tm'), may hold values from -0.375 to 0.375
- gate_x: bfloat16 [16, 2, 8, 256, 256], P('section', None, None, 'tm'), may hold values from -0.375 to 0.375
- bias_a: float32 [16, 2, 2048], P('section'), may hold values from -4 to 4
- bias_x: float32 [16, 2, 2048], P('section'), may hold values from -4 to 4
- rate_param: float32 [16, 2, 2048], P('section'), may hold values from -16 to -3.5, as said below
- norm_gain: float32 [16, 2, 2048], P('section'), may hold values from 0.5 to 1.5
- section_layers: int32 [16], P('section'), may hold values from 1 to 2
Outputs:
- acts_out: bfloat16 [16, 4096, 2048], P('section', 'tm')
- grad_out: bfloat16 [16, 4096, 2048], P('section', 'tm')
- grad_gain: float32 [16, 2, 2048], P('section')
- grad_bias_a: float32 [16, 2, 2048], P('section')
- grad_bias_x: float32 [16, 2, 2048], P('section')
- grad_rate: float32 [16, 2, 2048], P('section')
Inputs may be any that keep to these rules, and one draw needn't show every extreme that they name: `rate_param`: softplus of every entry lies between 0.05 / 4096 and 0.02.
All inputs are finite; a program needn't handle non-finite values.
Results may differ from a plain program's by a relative error of at most 0.015.
Values may be sent and summed in bfloat16 or wider, within the bound.
A program may use at most 192 MiB of HBM per device.

v0:
```python
import functools

import jax
import jax.numpy as jnp
from jax import lax
from jax.sharding import Mesh
from jax.sharding import PartitionSpec as P

TM = ("tm_0", "tm_1")


EPS = 1e-06


def in_one_piece(arrays, axis, dim, along):
    ends, at = ([], 0)
    for a in arrays[:-1]:
        at += a.shape[along]
        ends.append(at)
    both = jnp.concatenate(arrays, axis=along)
    return tuple(jnp.split(lax.all_gather(both, axis, axis=dim, tiled=True), ends, axis=along))


def sent_to_all(shard, axis):
    copies = jnp.broadcast_to(shard, (lax.axis_size(axis), *shard.shape))
    return lax.all_to_all(copies, axis, split_axis=0, concat_axis=0, tiled=True)


def gathered_once(shard, axis):
    leaves = jax.tree.leaves(shard)
    turns = sorted(range(len(leaves)), key=lambda k: -leaves[k].size)
    width = (1, *leaves[turns[0]].shape)[-1]
    lines = [
        jnp.pad(leaves[k].reshape(-1), (0, -leaves[k].size % width)).reshape(-1, width)
        for k in turns
    ]
    both, at, found = (sent_to_all(jnp.concatenate(lines), axis), 0, {})
    for k, line in zip(turns, lines):
        slab = both[:, at : at + len(line)].reshape(len(both), -1)
        found[k] = slab[:, : leaves[k].size].reshape(-1, *leaves[k].shape)
        at += len(line)
    numbers = iter(range(len(leaves)))
    return jax.tree.map(lambda _: found[next(numbers)], shard)


def joined_by_halves(pieces, combine):
    while len(jax.tree.leaves(pieces)[0]) > 1:
        pieces = jax.vmap(combine)(
            *(jax.tree.map(lambda part: part[side::2], pieces) for side in (0, 1))
        )
    return jax.tree.map(lambda part: part[0], pieces)


def prefix(shard, axis, combine, identity):
    size, mine = (lax.axis_size(axis), lax.axis_index(axis))
    passed = jnp.arange(size) < mine

    def prefix_kept(part, zero, own):
        part = jnp.where(
            passed.reshape(-1, *(1 for _ in own.shape)), part, jnp.asarray(zero, own.dtype)
        )
        return part

    pieces = gathered_once(shard, axis)
    return joined_by_halves(jax.tree.map(prefix_kept, pieces, identity, shard), combine)


def gathered_by_type(shard, axis):
    leaves, found = (jax.tree.leaves(shard), {})
    for initial, a in enumerate(leaves):
        if initial not in found:
            alike = [k for k, b in enumerate(leaves) if b.dtype == a.dtype]
            got = (
                gathered_once([leaves[k] for k in alike], axis)
                if len(alike) > 1
                else [sent_to_all(a, axis)]
            )
            for k, b in zip(alike, got):
                found[k] = b
    numbers = iter(range(len(leaves)))
    return jax.tree.map(lambda _: found[next(numbers)], shard)


def carried_in(shard, axis, combine, identity):
    size, mine = (lax.axis_size(axis), lax.axis_index(axis))
    passed = jnp.arange(size) > mine

    def carried_kept(part, zero, own):
        part = jnp.where(
            passed.reshape(-1, *(1 for _ in own.shape)), part, jnp.asarray(zero, own.dtype)
        )
        return part[::-1]

    pieces = gathered_by_type(shard, axis)
    return joined_by_halves(jax.tree.map(carried_kept, pieces, identity, shard), combine)


def from_behind(value, axis, steps):
    count = lax.axis_size(axis)
    pairs = [(source, (source + steps) % count) for source in range(count)]
    return lax.ppermute(value, axis, pairs)


def shortened(shard):
    return jax.tree.map(lambda a: a.astype(jnp.bfloat16) if a.dtype == jnp.float32 else a, shard)


def one_axis_at_a_time(shard, axes):
    return functools.reduce(lax.psum, axes, shard)


def combine(earlier, later):
    return (earlier[0] * later[0], later[0] * earlier[1] + later[1])


def local(
    acts_in,
    saved_in,
    grad_in,
    gate_a,
    gate_x,
    bias_a,
    bias_x,
    rate_param,
    norm_gain,
    section_layers,
):
    layer_count = section_layers[0]
    tok_rows = acts_in.shape[1]
    channels = acts_in.shape[2]
    head_count = gate_a.shape[2]
    block_size = gate_a.shape[4]
    slot_total = gate_a.shape[1]
    row_ids = lax.broadcasted_iota(jnp.int32, (tok_rows, tok_rows), 0)
    col_ids = lax.broadcasted_iota(jnp.int32, (tok_rows, tok_rows), 1)
    lower = (row_ids >= col_ids).astype(jnp.float32)
    upper = (row_ids <= col_ids).astype(jnp.float32)
    highest = lax.Precision.HIGHEST
    full_a, full_x = in_one_piece((gate_a, gate_x), TM, 3, 0)

    def mix_forward(inputs3, slot_index):
        weight_a = full_a[0, slot_index]
        weight_x = full_x[0, slot_index]
        first = jnp.einsum("thi,hio->tho", inputs3, weight_a, preferred_element_type=jnp.float32)
        second = jnp.einsum("thi,hio->tho", inputs3, weight_x, preferred_element_type=jnp.float32)
        return (first, second)

    def mix_backward(grads_a, grads_x, slot_index):
        weight_a = full_a[0, slot_index]
        weight_x = full_x[0, slot_index]
        first = jnp.einsum("tho,hio->thi", grads_a, weight_a, preferred_element_type=jnp.float32)
        return first + jnp.einsum(
            "tho,hio->thi", grads_x, weight_x, preferred_element_type=jnp.float32
        )

    def run_forward(x_in, slot_index, live_mask):
        stream_count = x_in.shape[0]
        x_float = x_in.astype(jnp.float32)
        mean_sq = jnp.mean(x_float * x_float, axis=-1, keepdims=True)
        inv_rms = lax.rsqrt(mean_sq + EPS)
        normed = x_float * inv_rms
        normed_in = (normed * norm_gain[0, slot_index]).astype(jnp.bfloat16)
        u_float = normed_in.astype(jnp.float32)
        flat_in = normed_in.reshape(stream_count * tok_rows, head_count, block_size)
        pre_a, pre_x = mix_forward(flat_in, slot_index)
        pre_a = pre_a.reshape(x_in.shape) + bias_a[0, slot_index]
        pre_x = pre_x.reshape(x_in.shape) + bias_x[0, slot_index]
        reset_gate = jax.nn.sigmoid(pre_a)
        input_gate = jax.nn.sigmoid(pre_x)
        decay_rate = jax.nn.softplus(rate_param[0, slot_index])
        log_decay = -8.0 * reset_gate * decay_rate
        decay = jnp.exp(log_decay)
        scaling = jnp.sqrt(-jnp.expm1(2.0 * log_decay))
        update = scaling * input_gate * u_float
        cum_log = jnp.einsum("ts,bsc->btc", lower, log_decay, precision=highest)
        grown = jnp.exp(cum_log)
        partial_value = jnp.einsum(
            "ts,bsc->btc", lower, jnp.exp(-cum_log) * update, precision=highest
        )
        local_states = grown * partial_value
        identity = (jnp.ones_like(grown[:, -1]), jnp.zeros_like(local_states[:, -1]))
        _, state_in = prefix((grown[:, -1], local_states[:, -1]), TM, combine, identity)
        states = local_states + grown * state_in[:, None, :]
        output = (x_float + live_mask * states).astype(jnp.bfloat16)
        stashed = (
            normed,
            inv_rms,
            u_float,
            reset_gate,
            input_gate,
            decay,
            scaling,
            states,
            state_in,
            cum_log,
        )
        return (output, tuple((piece[-1] for piece in stashed)))

    def run_backward(upstream, stashed, slot_index, live_mask):
        (
            normed,
            inv_rms,
            u_float,
            reset_gate,
            input_gate,
            decay,
            scaling,
            states,
            state_in,
            cum_log,
        ) = stashed
        decay_rate = jax.nn.softplus(rate_param[0, slot_index])
        d_state = live_mask * upstream
        grown = jnp.exp(cum_log)
        summed = jnp.einsum("ts,sc->tc", upper, grown * d_state, precision=highest)
        shrink = decay * jnp.exp(-cum_log)
        tail_z = shrink * summed
        tail_a = shrink * grown[-1][None, :]
        identity = (jnp.ones_like(tail_a[0]), jnp.zeros_like(tail_z[0]))
        _, z_enter = carried_in((tail_a[0], tail_z[0]), TM, combine, identity)
        z_full = tail_z + tail_a * z_enter[None, :]
        z_next = jnp.concatenate([z_full[1:], z_enter[None, :]], axis=0)
        adjoint = d_state + z_next
        h_prev = jnp.concatenate([state_in[None, :], states[:-1]], axis=0)
        d_decay = adjoint * h_prev
        d_input = adjoint * scaling * u_float
        d_log = d_decay * decay - adjoint * input_gate * u_float * decay * decay / scaling
        d_pre_a = d_log * (-8.0 * decay_rate) * reset_gate * (1.0 - reset_gate)
        d_pre_x = d_input * input_gate * (1.0 - input_gate)
        g_rate = jnp.sum(d_log * (-8.0 * reset_gate), axis=0) * jax.nn.sigmoid(
            rate_param[0, slot_index]
        )
        g_bias_a = jnp.sum(d_pre_a, axis=0)
        g_bias_x = jnp.sum(d_pre_x, axis=0)
        grads_a = d_pre_a.astype(jnp.bfloat16).reshape(tok_rows, head_count, block_size)
        grads_x = d_pre_x.astype(jnp.bfloat16).reshape(tok_rows, head_count, block_size)
        mixed = mix_backward(grads_a, grads_x, slot_index).reshape(tok_rows, channels)
        d_normed_in = adjoint * scaling * input_gate + mixed
        g_gain = jnp.sum(d_normed_in * normed, axis=0)
        d_normed = d_normed_in * norm_gain[0, slot_index]
        inner = jnp.mean(d_normed * normed, axis=-1, keepdims=True)
        downstream = upstream + inv_rms * (d_normed - normed * inner)
        return (downstream, (g_gain, g_bias_a, g_bias_x, g_rate))

    live_masks = [
        (slot_index < layer_count).astype(jnp.float32) for slot_index in range(slot_total)
    ]
    stash_list = []
    current = jnp.concatenate([acts_in, saved_in], axis=0)
    for slot_index in range(slot_total):
        current, stashed = run_forward(current, slot_index, live_masks[slot_index])
        stash_list.append(stashed)
    forwarded = current[0:1]
    acts_out = from_behind(forwarded, "section", 1)
    upstream = grad_in[0].astype(jnp.float32)
    grad_lists = [None] * slot_total
    for slot_index in reversed(range(slot_total)):
        upstream, slot_grads = run_backward(
            upstream, stash_list[slot_index], slot_index, live_masks[slot_index]
        )
        grad_lists[slot_index] = slot_grads
    partials = tuple(
        (jnp.stack([grad_lists[k][m] for k in range(slot_total)], axis=0) for m in range(4))
    )
    g_gain, g_bias_a, g_bias_x, g_rate = jax.tree.map(
        lambda part: part.astype(jnp.float32),
        jax.tree.map(lambda part: one_axis_at_a_time(part, TM), shortened(partials)),
    )
    grad_out = from_behind(upstream.astype(jnp.bfloat16)[None], "section", -1)
    return (acts_out, grad_out, g_gain[None], g_bias_a[None], g_bias_x[None], g_rate[None])


def solution(mesh):
    finer = Mesh(mesh.devices.reshape(mesh.shape["section"], 4, 8), ("section", "tm_0", "tm_1"))
    return jax.shard_map(
        local,
        mesh=finer,
        in_specs=(
            P("section", TM, None),
            P("section", TM, None),
            P("section", TM, None),
            P("section", None, None, TM, None),
            P("section", None, None, TM, None),
            P("section", None, None),
            P("section", None, None),
            P("section", None, None),
            P("section", None, None),
            P("section"),
        ),
        out_specs=(
            P("section", TM, None),
            P("section", TM, None),
            P("section", None, None),
            P("section", None, None),
            P("section", None, None),
            P("section", None, None),
        ),
        check_vma=False,
    )
```

profile of v0, /device:TPU:4, one launch (start us, length us, event | category | flops | bytes accessed | tf_op | source)
XLA Modules:
  0.0 447.0 jit_solution(4421518191950927114)
XLA Ops:
  13.3 88.4 %all-gather.2.cloned.1.call-done = bf16[2,2,8,256,256]{4,2,1,0,3:T(8,128)(2,1)} async-done(((bf16[2,2,8,8,256]{4,2,1,0,3:T(8,128)(2,1)}), bf16[2,2,8,256,256]{4,2,1,0,3:T(8,128)(2,1)}) %all-gather.2.cloned.1.call-update) | async-done | bytes 4194320 | tf_op jit(solution)/shard_map/all_gather | solution.py:21
  101.8 4.3 fusion.135
  114.7 5.2 %negate_sqrt_fusion.1 = (f32[2,128,2048]{2,1,0:T(8,128)}, f32[2,128,2048]{2,1,0:T(8,128)S(1)}, f32[2,128,2048]{2,1,0:T(8,128)}) fusion(f32[2048]{0:T(1024)S(1)} %bitcast.422, f32[2,128,2048]{2,1,0:T(8,128)} %copy.291, f32[2048]{0:T(1024)S(1)} %bitcast.420), kind=kLoop, calls=%fused_computation.29 | loop fusion | flops 3670016 | bytes 8404992 | tf_op jit(solution)/shard_map/sqrt | solution.py:173
  119.9 3.4 fusion.148
  124.9 4.3 convolution_bitcast_fusion.6
  132.4 4.2 copy.292
  146.0 8.2 %all-to-all-start = ((f32[32,4,2048]{2,1,0:T(4,128)}), f32[32,4,2048]{2,1,0:T(4,128)}, u32[]{:S(2)}, u32[]{:S(2)}) async-start(f32[32,4,2048]{2,1,0:T(4,128)} %broadcast_in_dim.98), calls=%async_computation | async-start | bytes 2097152 | tf_op jit(solution)/shard_map/all_to_all | solution.py:26
  180.3 3.9 convert_multiply_fusion
  195.8 5.3 %negate_sqrt_fusion = (f32[2,128,2048]{2,1,0:T(8,128)}, f32[2,128,2048]{2,1,0:T(8,128)S(1)}, f32[2,128,2048]{2,1,0:T(8,128)}) fusion(f32[2048]{0:T(1024)S(1)} %bitcast.421, f32[2,128,2048]{2,1,0:T(8,128)} %copy.293, f32[2048]{0:T(1024)S(1)} %bitcast.419), kind=kLoop, calls=%fused_computation.16 | loop fusion | flops 3670016 | bytes 8404992 | tf_op jit(solution)/shard_map/sqrt | solution.py:173
  201.1 3.4 fusion.149
  208.2 3.3 reshape.467
  211.5 4.6 %copy.294 = f32[2,128,2048]{2,1,0:T(8,128)} copy(f32[2,128,2048]{1,0,2:T(2,128)} %reshape.467) | data formatting | bytes 4194304 | tf_op jit(solution)/shard_map/reshape | solution.py:167
  221.4 9.3 %all-to-all-start.2 = ((f32[32,2,2048]{2,1,0:T(2,128)}), f32[32,2,2048]{2,1,0:T(2,128)}, u32[]{:S(2)}, u32[]{:S(2)}) async-start(f32[32,2,2048]{2,1,0:T(2,128)} %broadcast_in_dim.103), calls=%async_computation.2 | async-start | bytes 1048576 | tf_op jit(solution)/shard_map/all_to_all | solution.py:26
  262.7 10.2 %all-to-all-start.1 = ((f32[32,4,2048]{2,1,0:T(4,128)}), f32[32,4,2048]{2,1,0:T(4,128)}, u32[]{:S(2)}, u32[]{:S(2)}) async-start(f32[32,4,2048]{2,1,0:T(4,128)} %broadcast_in_dim.101), calls=%async_computation.1 | async-start | bytes 2097152 | tf_op jit(solution)/shard_map/all_to_all | solution.py:26
  286.1 8.7 %all-to-all-done.1 = f32[32,4,2048]{2,1,0:T(4,128)} async-done(((f32[32,4,2048]{2,1,0:T(4,128)}), f32[32,4,2048]{2,1,0:T(4,128)}, u32[]{:S(2)}, u32[]{:S(2)}) %all-to-all-start.1) | async-done | bytes 1048608 | tf_op jit(solution)/shard_map/all_to_all | solution.py:26
  308.3 5.0 %fusion.81 = f32[8,256,128]{2,1,0:T(8,128)S(1)} fusion(bf16[1,1,8,256,256]{3,4,2,1,0:T(8,128)(2,1)} %copy.318, f32[128,8,256]{0,2,1:T(8,128)} %bitcast.388, f32[128,8,256]{0,2,1:T(8,128)} %bitcast.358, f32[128,8,256]{0,2,1:T(8,128)} %bitcast.387, f32[128,8,256]{0,2,1:T(8,128)} %bitcast.376, f32[128,8,256]{0,2,1:T(8,128)} %maximum_add_fusion.1, ...), kind=kOutput, calls=%fused_computation.160 | convolution fusion | flops 137887744 | bytes 9445376 | tf_op jit(solution)/shard_map/tho,hio->thi/dot_general | solution.py:151
  325.7 8.0 %all-to-all-start.3 = ((f32[32,2,2048]{2,1,0:T(2,128)}), f32[32,2,2048]{2,1,0:T(2,128)}, u32[]{:S(2)}, u32[]{:S(2)}) async-start(f32[32,2,2048]{2,1,0:T(2,128)} %broadcast_in_dim.106), calls=%async_computation.3 | async-start | bytes 1048576 | tf_op jit(solution)/shard_map/all_to_all | solution.py:26
  345.1 3.3 collective-permute-done
  355.9 3.5 fusion.63
  364.1 3.7 maximum_add_fusion.4
  375.2 4.8 %fusion.25 = (f32[128,2048]{1,0:T(8,128)}, f32[128,2048]{1,0:T(8,128)S(1)}) fusion(f32[128,2048]{1,0:T(8,128)} %get-tuple-element.27, f32[127,2048]{1,0:T(8,128)} %get-tuple-element.53, f32[1,2048]{1,0:T(1,128)S(1)} %copy-done.78, f32[2,128,2048]{2,1,0:T(8,128)} %get-tuple-element.58, f32[2,128,2048]{2,1,0:T(8,128)} %copy-done.12, ...), kind=kLoop, calls=%fused_computation.56 | loop fusion | flops 3145728 | bytes 9437184 | tf_op jit(solution)/shard_map/sub | solution.py:227
  383.0 5.7 %fusion.46 = bf16[1,128,2048]{2,1,0:T(8,128)(2,1)} fusion(f32[1,128,2048]{2,1,0:T(8,128)} %copy.300, f32[1,1,2048]{2,1,0:T(1,128)S(1)} %bitcast.404, f32[1,127,2048]{2,1,0:T(8,128)} %bitcast.364, f32[1,128,2048]{2,1,0:T(8,128)} %copy.296, f32[1,1,2048]{2,1,0:T(1,128)S(1)} %bitcast.398, f32[1,127,2048]{2,1,0:T(8,128)S(1)} %bitcast.355, ...), kind=kLoop, calls=%fused_computation.91 | loop fusion | flops 6291456 | bytes 11552776 | tf_op jit(solution)/shard_map/convert_element_type | solution.py:269
  389.7 15.5 %all-reduce.1 = (bf16[2,2048]{1,0:T(2,128)(2,1)S(1)}, bf16[2,2048]{1,0:T(2,128)(2,1)S(1)}, bf16[2,2048]{1,0:T(2,128)(2,1)S(1)}, bf16[2,2048]{1,0:T(2,128)(2,1)S(1)}) all-reduce(bf16[2,2048]{1,0:T(2,128)(2,1)S(1)} %pad_maximum_fusion.6, ...), channel_id=1, replica_groups=mesh['section'=16,'tm_0'=4,'tm_1'=8] {'tm_0'}, use_global_device_ids=true, to_apply=%region_6.7 | all-reduce | flops 16384 | bytes 65536 | tf_op jit(solution)/shard_map/psum | solution.py:109
  405.2 29.6 %all-reduce = (bf16[1,2,2048]{2,1,0:T(2,128)(2,1)S(1)}, bf16[1,2,2048]{2,1,0:T(2,128)(2,1)S(1)}, bf16[1,2,2048]{2,1,0:T(2,128)(2,1)S(1)}, bf16[1,2,2048]{2,1,0:T(2,128)(2,1)S(1)}) all-reduce(bf16[1,2,2048]{2,1,0:T(2,128)(2,1)S(1)} %bitcast.423, ...), channel_id=1, replica_groups=mesh['section'=16,'tm_0'=4,'tm_1'=8] {'tm_1'}, use_global_device_ids=true, to_apply=%region_7.8 | all-reduce | flops 16384 | bytes 65536 | tf_op jit(solution)/shard_map/psum | solution.py:109
  (387 shorter events, 184.7 us)
Async XLA Ops:
  7.2 94.6 %all-gather.2.cloned.1.call-start = ((), (), s32[]{:S(2)}) async-start(), calls=%async_computation.4 | async-start | bytes 4325376 | tf_op jit(solution)/shard_map/all_gather | solution.py:21
  9.7 170.6 %copy-start.67 = (f32[1,1,2048]{2,1,0:T(1,128)}, f32[1,1,2048]{2,1,0:T(1,128)S(1)}, u32[]{:S(2)}) copy-start(f32[1,1,2048]{2,1,0:T(1,128)S(1)} %get-tuple-element.115) | copy-start | bytes 24580
  12.0 95.9 %copy-start.19 = (f32[32,8,8,256]{3,2,1,0:T(8,128)}, f32[32,8,8,256]{3,2,1,0:T(8,128)S(1)}, u32[]{:S(2)}) copy-start(f32[32,8,8,256]{3,2,1,0:T(8,128)S(1)} %copy.325) | copy-start | bytes 6291460
  119.9 44.5 %copy-start = (f32[2,128,2048]{2,1,0:T(8,128)}, f32[2,128,2048]{2,1,0:T(8,128)S(1)}, u32[]{:S(2)}) copy-start(f32[2,128,2048]{2,1,0:T(8,128)S(1)} %get-tuple-element.40) | copy-start | bytes 6291460
  142.4 12.5 %copy-start.16 = (bf16[1,128,2048]{2,1,0:T(8,128)(2,1)S(1)}, bf16[1,128,2048]{2,1,0:T(8,128)(2,1)}, u32[]{:S(2)}) copy-start(bf16[1,128,2048]{2,1,0:T(8,128)(2,1)} %param.12) | copy-start | bytes 1572868
  146.0 31.4 %all-to-all-start = ((f32[32,4,2048]{2,1,0:T(4,128)}), f32[32,4,2048]{2,1,0:T(4,128)}, u32[]{:S(2)}, u32[]{:S(2)}) async-start(f32[32,4,2048]{2,1,0:T(4,128)} %broadcast_in_dim.98), calls=%async_computation | async-start | bytes 2097152 | tf_op jit(solution)/shard_map/all_to_all | solution.py:26
  221.4 40.0 %all-to-all-start.2 = ((f32[32,2,2048]{2,1,0:T(2,128)}), f32[32,2,2048]{2,1,0:T(2,128)}, u32[]{:S(2)}, u32[]{:S(2)}) async-start(f32[32,2,2048]{2,1,0:T(2,128)} %broadcast_in_dim.103), calls=%async_computation.2 | async-start | bytes 1048576 | tf_op jit(solution)/shard_map/all_to_all | solution.py:26
  243.1 4.9 %slice-start = ((f32[2,128,2048]{2,1,0:T(8,128)}), f32[1,128,2048]{2,1,0:T(8,128)S(1)}, s32[]{:S(2)}) async-start(f32[2,128,2048]{2,1,0:T(8,128)} %copy-done.9), calls=%async_computation.5 | async-start | bytes 2097152 | tf_op jit(solution)/shard_map/slice | solution.py:197
  261.5 59.3 %copy-start.81 = (f32[128]{0:T(128)}, f32[128]{0:T(128)S(1)}, u32[]{:S(2)}) copy-start(f32[128]{0:T(128)S(1)} %get-tuple-element.129) | copy-start | bytes 1540
  262.7 32.1 %all-to-all-start.1 = ((f32[32,4,2048]{2,1,0:T(4,128)}), f32[32,4,2048]{2,1,0:T(4,128)}, u32[]{:S(2)}, u32[]{:S(2)}) async-start(f32[32,4,2048]{2,1,0:T(4,128)} %broadcast_in_dim.101), calls=%async_computation.1 | async-start | bytes 2097152 | tf_op jit(solution)/shard_map/all_to_all | solution.py:26
  308.3 5.1 %copy-start.21 = (f32[128,8,256]{0,2,1:T(8,128)S(1)}, f32[128,8,256]{0,2,1:T(8,128)}, u32[]{:S(2)}) copy-start(f32[128,8,256]{0,2,1:T(8,128)} %maximum_add_fusion.1) | copy-start | bytes 3145732
  308.3 5.1 %copy-start.23 = (f32[1,128,2048]{1,2,0:T(8,128)S(1)}, f32[1,128,2048]{1,2,0:T(8,128)}, u32[]{:S(2)}) copy-start(f32[1,128,2048]{1,2,0:T(8,128)} %copy.306) | copy-start | bytes 3145732
  308.3 5.1 %copy-start.25 = (f32[1,128,2048]{1,2,0:T(8,128)S(1)}, f32[1,128,2048]{1,2,0:T(8,128)}, u32[]{:S(2)}) copy-start(f32[1,128,2048]{1,2,0:T(8,128)} %copy.304) | copy-start | bytes 3145732
  308.3 5.1 %copy-start.35 = (f32[1,128,2048]{1,2,0:T(8,128)S(1)}, f32[1,128,2048]{1,2,0:T(8,128)}, u32[]{:S(2)}) copy-start(f32[1,128,2048]{1,2,0:T(8,128)} %copy.305) | copy-start | bytes 3145732
  308.3 5.2 %copy-start.41 = (bf16[1,1,8,256,256]{3,4,2,1,0:T(8,128)(2,1)S(1)}, bf16[1,1,8,256,256]{3,4,2,1,0:T(8,128)(2,1)}, u32[]{:S(2)}) copy-start(bf16[1,1,8,256,256]{3,4,2,1,0:T(8,128)(2,1)} %copy.319) | copy-start | bytes 3145732
  325.7 22.6 %all-to-all-start.3 = ((f32[32,2,2048]{2,1,0:T(2,128)}), f32[32,2,2048]{2,1,0:T(2,128)}, u32[]{:S(2)}, u32[]{:S(2)}) async-start(f32[32,2,2048]{2,1,0:T(2,128)} %broadcast_in_dim.106), calls=%async_computation.3 | async-start | bytes 1048576 | tf_op jit(solution)/shard_map/all_to_all | solution.py:26
  338.2 10.1 %collective-permute-start = (bf16[1,128,2048]{2,1,0:T(8,128)(2,1)}, bf16[1,128,2048]{2,1,0:T(8,128)(2,1)}, u32[]{:S(2)}, u32[]{:S(2)}) collective-permute-start(bf16[1,128,2048]{2,1,0:T(8,128)(2,1)} %fusion.30), channel_id=1, source_target_pairs={{0,32},{32,64},{64,96},{96,128},{128,160},{160,192},{192,224},{224... | collective-permute-start | bytes 1572872 | tf_op jit(solution)/shard_map/ppermute | solution.py:101
  364.0 4.9 %copy-start.63 = (f32[1,127,2048]{1,2,0:T(8,128)S(1)}, f32[1,127,2048]{1,2,0:T(8,128)}, u32[]{:S(2)}) copy-start(f32[1,127,2048]{1,2,0:T(8,128)} %copy.261) | copy-start | bytes 3121156
  364.0 5.2 %copy-start.64 = (f32[1,8,256]{0,2,1:T(8,128)S(1)}, f32[1,8,256]{0,2,1:T(8,128)}, u32[]{:S(2)}) copy-start(f32[1,8,256]{0,2,1:T(8,128)} %concatenate.107) | copy-start | bytes 24580
  364.0 5.2 %copy-start.76 = (f32[8,256]{1,0:T(8,128)S(1)}, f32[8,256]{1,0:T(8,128)}, u32[]{:S(2)}) copy-start(f32[8,256]{1,0:T(8,128)} %fusion.112) | copy-start | bytes 24580
  383.0 5.7 %copy-start.55 = (f32[2,128,2048]{2,1,0:T(8,128)S(1)}, f32[2,128,2048]{2,1,0:T(8,128)}, u32[]{:S(2)}) copy-start(f32[2,128,2048]{2,1,0:T(8,128)} %get-tuple-element.41) | copy-start | bytes 6291460
  383.0 5.7 %copy-start.66 = (f32[128,2048]{1,0:T(8,128)S(1)}, f32[128,2048]{1,0:T(8,128)}, u32[]{:S(2)}) copy-start(f32[128,2048]{1,0:T(8,128)} %get-tuple-element.47) | copy-start | bytes 3145732
  383.0 5.7 %copy-start.71 = (f32[2048]{0:T(1024)S(1)}, f32[2048]{0:T(1024)}, u32[]{:S(2)}) copy-start(f32[2048]{0:T(1024)} %fusion.113) | copy-start | bytes 24580
  388.7 48.5 %collective-permute-start.1 = (bf16[1,128,2048]{2,1,0:T(8,128)(2,1)}, bf16[1,128,2048]{2,1,0:T(8,128)(2,1)S(1)}, u32[]{:S(2)}, u32[]{:S(2)}) collective-permute-start(bf16[1,128,2048]{2,1,0:T(8,128)(2,1)} %fusion.46), channel_id=1, source_target_pairs={{0,480},{32,0},{64,32},{96,64},{128,96},{160,128},{192,160},{224,1... | collective-permute-start | bytes 1572872 | tf_op jit(solution)/shard_map/ppermute | solution.py:101
  (71 other events, 185.8 us)
Sparse Core Ops, SparseCore 0:
  11.7 89.9 all-gather.1
where the time goes:
time: 451 us; the launch traced here: 447 us
  local copies, waits for them, and re-layouts  139 us (31%)
  waiting for transfers between devices  101 us (22%)
  other arithmetic  73.5 us (16%)
  blocking collectives  45.1 us (10%)
  starting transfers between devices  35.8 us (8%)
  matrix products  35.6 us (8%)
  between operations  16.5 us (4%)
    all_gather x1, waiting for transfers between devices, in_one_piece(): lax.all_gather(both, axis, axis=dim, tiled=True)  88.4 us
    psum x2, blocking collectives, one_axis_at_a_time(): return functools.reduce(lax.psum, axes, shard)  45.1 us
    all_to_all x4, starting transfers between devices, sent_to_all(): return lax.all_to_all(copies, axis, split_axis=0, concat_axis=0, tiled=True)  35.7 us
    unnamed x184, local copies, waits for them, and re-layouts  27.1 us
    squeeze x11, local copies, waits for them, and re-layouts, run_forward(): return (output, tuple((piece[-1] for piece in stashed)))  19.6 us
    reshape x4, local copies, waits for them, and re-layouts, run_forward(): pre_x = pre_x.reshape(x_in.shape) + bias_x[0, slot_index]  15.3 us
    sqrt x2, other arithmetic, run_forward(): scaling = jnp.sqrt(-jnp.expm1(2.0 * log_decay))  10.5 us
    slice x12, local copies, waits for them, and re-layouts, run_forward(): return (output, tuple((piece[-1] for piece in stashed)))  10.4 us
  transfers between devices with their start and end apart: 7, of which 4 were waited for; matrix products, arithmetic and copies ran while one was open for 18% of the time, Pallas kernels for 0%

commit v1 on v0

v1 whole, which is shorter than its diff:
```python
import jax
import jax.numpy as jnp
from jax import lax
from jax.experimental import pallas as pl
from jax.experimental.pallas import tpu as pltpu
from jax.sharding import Mesh
from jax.sharding import PartitionSpec as P

MESH = pl.DeviceIdType.MESH
F32, BF16 = jnp.float32, jnp.bfloat16
EPS = 1e-06
NX, NY = 4, 8
GROUPS, LANES8 = 16, 8
BLK = 256
STEP = 4
PER_LAYER = 43


def kernel(
    acts_hbm, saved_hbm, grad_hbm, ga_hbm, gx_hbm, bias_a, bias_x, rate_param, gain, layers,
    acts_out, grad_out, o_gain, o_ba, o_bx, o_rate,
    wa, wx, wfull, xin, out_buf,
    x0, x1, inv, ac, hl, st_a, st_r, st_i, st_s, st_rs, qp, bn, dy, dn,
    pre_a, pre_x, ends, par, gsum,
    ey0, ex0, ey1, ex1, ey2, ex2, eyg, exg,
    load_sem, g_send, g_recv, e_send, e_recv, o_send, o_recv,
):
    s, mx, my = lax.axis_index("section"), lax.axis_index("tm_0"), lax.axis_index("tm_1")
    ns = lax.axis_size("section")
    heads = x0.shape[-1] // BLK
    chans = x0.shape[-1]
    pieces = chans // 128

    def xp(d):
        return lax.rem(mx + (d + NX), NX)

    def yp(d):
        return lax.rem(my + (d + NY), NY)

    def at_x(d):
        return (s, xp(d), my)

    def at_y(d):
        return (s, mx, yp(d))

    sec_next = (lax.rem(s + 1, ns), mx, my)
    sec_prev = (lax.rem(s + (ns - 1), ns), mx, my)

    loads = [
        pltpu.make_async_copy(ga_hbm, wa.at[:, mx, my], load_sem.at[0]),
        pltpu.make_async_copy(gx_hbm, wx.at[:, mx, my], load_sem.at[1]),
        pltpu.make_async_copy(saved_hbm, xin.at[0], load_sem.at[2]),
        pltpu.make_async_copy(acts_hbm, xin.at[1], load_sem.at[3]),
        pltpu.make_async_copy(grad_hbm, xin.at[2], load_sem.at[4]),
    ]
    for c in loads:
        c.start()

    barrier = pltpu.get_barrier_semaphore()
    peers = [at_y(d) for d in range(1, NY)] + [at_x(d) for d in range(1, NX)]
    peers += [sec_next, sec_prev]
    for dev in peers:
        pl.semaphore_signal(barrier, inc=1, device_id=dev, device_id_type=MESH)
    pl.semaphore_wait(barrier, len(peers))

    sent = []

    def send(src, dst, sems, k, dev):
        c = pltpu.make_async_remote_copy(
            src_ref=src, dst_ref=dst, send_sem=sems[0].at[k], recv_sem=sems[1].at[k],
            device_id=dev, device_id_type=MESH,
        )
        c.start()
        sent.append(c)

    def arrived(slot, sems, k):
        pltpu.make_async_remote_copy(
            src_ref=slot, dst_ref=slot, send_sem=sems[0].at[k], recv_sem=sems[1].at[k],
            device_id=sec_next, device_id_type=MESH,
        ).wait_recv()

    gsems = (g_send, g_recv)

    def gather(l):
        base = l * PER_LAYER
        kx = lambda d: base + d - 1
        ka = lambda step, side: base + 3 + (step - 1) * 2 + side
        ky = lambda step, side: base + 11 + (step - 1) * 2 + side
        k1 = lambda d, up, side: base + 19 + (0 if d == 0 else (14 if d == 4 else 2 + (d - 1) * 4 + 2 * up)) + side
        k2 = lambda d, up: base + 35 + (0 if d == 0 else (7 if d == 4 else 1 + (d - 1) * 2 + up))

        def go(ref, k, dev):
            send(ref, ref, gsems, k, dev)

        def a_col(y):
            return wa.at[l, :, y]

        def x_piece(x, y):
            return wx.at[l, x, y]

        def x_first(d):
            for up in (0, 1) if d in (1, 2, 3) else (0,):
                y = yp(d if up else -d)
                go(x_piece(mx, y), k1(d, up, 0), at_x(1))
                go(x_piece(mx, y), k1(d, up, 1), at_x(-1))

        def x_first_in(d):
            for up in (0, 1) if d in (1, 2, 3) else (0,):
                y = yp(d if up else -d)
                arrived(x_piece(xp(-1), y), gsems, k1(d, up, 0))
                arrived(x_piece(xp(1), y), gsems, k1(d, up, 1))

        def x_second(d):
            if d != 4:
                go(x_piece(xp(-1), yp(-d)), k2(d, 0), at_x(1))
            if d != 0:
                go(x_piece(xp(1), yp(d)), k2(d, 1 if d != 4 else 0), at_x(-1))

        def x_second_in(d):
            if d != 4:
                arrived(x_piece(xp(2), yp(-d)), gsems, k2(d, 0))
            if d != 0:
                arrived(x_piece(xp(2), yp(d)), gsems, k2(d, 1 if d != 4 else 0))

        half = heads // 2
        lo, hi = slice(0, half), slice(half, heads)
        for d in (1, 3, 2):
            go(wa.at[l, mx, my], kx(d), at_x(d))
        go(x_piece(mx, my), ky(1, 0), at_y(1))
        go(x_piece(mx, my), ky(1, 1), at_y(-1))
        x_first(0)
        yield
        for d in (1, 3, 2):
            arrived(wa.at[l, xp(-d), my], gsems, kx(d))
        go(a_col(my), ka(1, 0), at_y(1))
        go(a_col(my), ka(1, 1), at_y(-1))
        for d in (1, 2, 3):
            if d > 1:
                arrived(a_col(yp(-(d - 1))), gsems, ka(d - 1, 0))
                go(a_col(yp(-(d - 1))), ka(d, 0), at_y(1))
                arrived(a_col(yp(d - 1)), gsems, ka(d - 1, 1))
                go(a_col(yp(d - 1)), ka(d, 1), at_y(-1))
            arrived(x_piece(mx, yp(-d)), gsems, ky(d, 0))
            arrived(x_piece(mx, yp(d)), gsems, ky(d, 1))
            if d < 3:
                go(x_piece(mx, yp(-d)), ky(d + 1, 0), at_y(1))
                go(x_piece(mx, yp(d)), ky(d + 1, 1), at_y(-1))
            else:
                go(wx.at[l, mx, yp(-3), lo], ky(4, 0), at_y(1))
                go(wx.at[l, mx, yp(3), hi], ky(4, 1), at_y(-1))
            x_first(d)
            x_first_in(d - 1)
            x_second(d - 1)
            yield
        arrived(a_col(yp(-3)), gsems, ka(3, 0))
        go(wa.at[l, :, yp(-3), lo], ka(4, 0), at_y(1))
        arrived(a_col(yp(3)), gsems, ka(3, 1))
        go(wa.at[l, :, yp(3), hi], ka(4, 1), at_y(-1))
        arrived(wx.at[l, mx, yp(4), lo], gsems, ky(4, 0))
        arrived(wx.at[l, mx, yp(4), hi], gsems, ky(4, 1))
        x_first(4)
        x_first_in(3)
        x_second(3)
        yield
        x_first_in(4)
        x_second(4)
        for d in (0, 1, 2, 3):
            x_second_in(d)
        yield
        arrived(wa.at[l, :, yp(4), lo], gsems, ka(4, 0))
        arrived(wa.at[l, :, yp(4), hi], gsems, ka(4, 1))
        x_second_in(4)

    esems = (e_send, e_recv)

    class Exchange:
        def __init__(self, number, yb, xb):
            self.base, self.yb, self.xb = number * (NX + NY - 2), yb, xb

        def y_start(self):
            for d in range(1, NY):
                send(self.yb.at[my], self.yb.at[my], esems, self.base + d - 1, at_y(d))

        def y_wait(self):
            for d in range(1, NY):
                arrived(self.yb.at[yp(-d)], esems, self.base + d - 1)

        def x_start(self):
            for d in range(1, NX):
                send(self.xb.at[mx], self.xb.at[mx], esems, self.base + NY - 1 + d - 1, at_x(d))

        def x_wait(self):
            for d in range(1, NX):
                arrived(self.xb.at[xp(-d)], esems, self.base + NY - 1 + d - 1)

    e0 = [Exchange(k, ey0.at[k], ex0.at[k]) for k in (0, 1)]
    e1 = Exchange(2, ey1, ex1)
    e1a = Exchange(3, ey2.at[0], ex2.at[0])
    e2 = Exchange(4, ey2.at[1, :, 0:1], ex2.at[1, :, 0:1])
    eg = [Exchange(5 + l, eyg.at[l], exg.at[l]) for l in (0, 1)]

    y = jnp.exp(rate_param[...])
    rate = y * (1.0 + y * (-1.0 / 2 + y * (1.0 / 3 + y * (-1.0 / 4 + y * (1.0 / 5 + y * (-1.0 / 6))))))
    par[0] = -8.0 * rate
    par[1] = y / (1.0 + y)
    live = [jnp.minimum(jnp.maximum(layers[0] - l, 0), 1).astype(F32) for l in (0, 1)]

    tok = lax.broadcasted_iota(jnp.int32, (128, 128), 1)
    row = lax.broadcasted_iota(jnp.int32, (128, 128), 0)
    to_runs = (tok == (row % LANES8) * GROUPS + row // LANES8).astype(F32).astype(BF16)
    to_tokens = (row == (tok % LANES8) * GROUPS + tok // LANES8).astype(F32).astype(BF16)
    sub = lax.broadcasted_iota(jnp.int32, (LANES8, chans), 0)

    def cols_of(h):
        return pl.ds(pl.multiple_of(h * BLK, BLK), BLK)

    def over_heads(body, lo=0, hi=None):
        def step(h, _):
            body(h, cols_of(h))
            return 0

        lax.fori_loop(lo, heads if hi is None else hi, step, 0)

    def chunks():
        return [pl.ds(c * STEP, STEP) for c in range(GROUPS // STEP)]

    def runs3(v):
        return v.reshape(GROUPS, LANES8, v.shape[-1])

    def rows2(v):
        return v.reshape(GROUPS * LANES8, v.shape[-1])

    def squares(x):
        sq = x * x
        return sq[..., :128] + sq[..., 128:]

    def store_inv(slot, acc):
        mean = jnp.sum(acc, axis=-1, keepdims=True) * (1.0 / chans)
        inv[slot] = jnp.broadcast_to(lax.rsqrt(mean + EPS), inv.shape[1:])

    def permuted(k, dst):
        def step(h, acc):
            cols = cols_of(h)
            x = runs3(jnp.dot(to_runs, xin[k, :, cols], preferred_element_type=F32))
            dst[:, :, cols] = x
            return acc + squares(x)

        return lax.fori_loop(0, heads, step, jnp.zeros((GROUPS, LANES8, 128), F32))

    def sigmoid(v):
        return 1.0 / (1.0 + jnp.exp(-v))

    def forward(l, stream, xref, kk, sl, build, lo, hi):
        def body(h, cols):
            g = gain[pl.ds(l, 1), cols]
            ba, bx = bias_a[pl.ds(l, 1), cols], bias_x[pl.ds(l, 1), cols]
            k8 = par[0, pl.ds(l, 1), cols]
            if build:
                w_a = wa[l, :, :, h].astype(F32).reshape(BLK, BLK).astype(BF16)
                w_x = wx[l, :, :, h].astype(F32).reshape(BLK, BLK).astype(BF16)
                wfull[l, 0, h] = w_a
                wfull[l, 1, h] = w_x
            else:
                w_a, w_x = wfull[l, 0, h], wfull[l, 1, h]
            u = rows2(xref[:, :, cols] * inv[kk] * g).astype(BF16)
            pre_a[...] = runs3(jnp.dot(u, w_a, preferred_element_type=F32))
            pre_x[...] = runs3(jnp.dot(u, w_x, preferred_element_type=F32))
            cum_a = jnp.ones((LANES8, BLK), F32)
            cum_h = jnp.zeros((LANES8, BLK), F32)
            for c, rows in enumerate(chunks()):
                uf = (xref[rows, :, cols] * inv[kk, rows] * g).astype(BF16).astype(F32)
                r = sigmoid(pre_a[rows] + ba)
                i = sigmoid(pre_x[rows] + bx)
                log_a = r * k8
                a = jnp.exp(log_a)
                z = log_a * 2.0
                p = 1.0 / 120 + z * (1.0 / 720)
                p = 1.0 / 24 + z * p
                p = 1.0 / 6 + z * p
                p = 0.5 + z * p
                p = 1.0 + z * p
                w = -(z * p)
                rs = lax.rsqrt(jnp.maximum(w, 1e-36))
                sc = w * rs
                up = sc * i * uf
                if stream == 0:
                    st_a[l, rows, :, cols] = a
                    st_r[l, rows, :, cols] = r
                    st_i[l, rows, :, cols] = i
                    st_s[l, rows, :, cols] = sc
                    st_rs[l, rows, :, cols] = rs
                for t in range(STEP):
                    cum_a = cum_a * a[t]
                    cum_h = a[t] * cum_h + up[t]
                    ac[sl, c * STEP + t + 1, :, cols] = cum_a
                    hl[sl, c * STEP + t + 1, :, cols] = cum_h
            ac[sl, 0, :, cols] = jnp.ones((LANES8, BLK), F32)
            hl[sl, 0, :, cols] = jnp.zeros((LANES8, BLK), F32)

        over_heads(body, lo, hi)

    def shifted(v, n, fill):
        if n > 0:
            return jnp.where(sub >= n, pltpu.roll(v, n, 0), fill)
        return jnp.where(sub < LANES8 + n, pltpu.roll(v, LANES8 + n, 0), fill)

    def joined(a, h, sign):
        for n in (1, 2, 4):
            h = a * shifted(h, sign * n, 0.0) + h
            a = a * shifted(a, sign * n, 1.0)
        return a, h

    def put_summary(dst, k, full, at):
        for g in range(pieces):
            dst[my, k, g : g + 1, :] = full[at : at + 1, 128 * g : 128 * (g + 1)]

    def summarise(sl, dst):
        a, h = joined(ac[sl, GROUPS], hl[sl, GROUPS], 1)
        ends[sl, 0] = shifted(a, 1, 1.0)
        ends[sl, 1] = shifted(h, 1, 0.0)
        put_summary(dst, 0, a, LANES8 - 1)
        put_summary(dst, 1, h, LANES8 - 1)

    def summarise_back(l, dst, k):
        a, z = joined(bn[l, GROUPS], qp[l, GROUPS], -1)
        ends[3 + l, 0] = shifted(a, -1, 1.0)
        ends[3 + l, 1] = shifted(z, -1, 0.0)
        put_summary(dst, k, z, 0)

    def row_total(yb, xb):
        a, h = yb[0, 0], yb[0, 1]
        for t in range(1, NY):
            h = yb[t, 0] * h + yb[t, 1]
            a = yb[t, 0] * a
        xb[mx, 0] = a
        xb[mx, 1] = h

    def row_total_back(ya, yz, kz, xz, kx):
        z = yz[NY - 1, kz]
        for t in reversed(range(NY - 1)):
            z = ya[t, 0] * z + yz[t, kz]
        xz[mx, kx] = z

    def entering(yb, xb):
        h = jnp.zeros((pieces, 128), F32)
        for t in range(NX - 1):
            h = jnp.where(t < mx, xb[t, 0] * h + xb[t, 1], h)
        for t in range(NY - 1):
            h = jnp.where(t < my, yb[t, 0] * h + yb[t, 1], h)
        return h

    def entering_back(ya, xa, yz, xz, kz):
        z = jnp.zeros((pieces, 128), F32)
        for t in reversed(range(1, NX)):
            z = jnp.where(t > mx, xa[t, 0] * z + xz[t, kz], z)
        for t in reversed(range(1, NY)):
            z = jnp.where(t > my, ya[t, 0] * z + yz[t, kz], z)
        return z

    def put_entering(k, h):
        for g in range(pieces):
            c = slice(128 * g, 128 * (g + 1))
            ends[k, 2, :, c] = ends[k, 1, :, c] + ends[k, 0, :, c] * h[g : g + 1]

    def next_layer(src, sl, dst):
        def step(h, acc):
            cols = cols_of(h)
            c = ends[sl, 2, :, cols]
            out = []
            for k in range(GROUPS // STEP):
                rows, later = pl.ds(k * STEP, STEP), pl.ds(k * STEP + 1, STEP)
                st = hl[sl, later, :, cols] + ac[sl, later, :, cols] * c
                x = (src[rows, :, cols] + live[0] * st).astype(BF16).astype(F32)
                dst[rows, :, cols] = x
                out.append(squares(x))
            return acc + jnp.concatenate(out, axis=0)

        return lax.fori_loop(0, heads, step, jnp.zeros((GROUPS, LANES8, 128), F32))

    def last_layer(src, sl):
        def body(h, cols):
            c = ends[sl, 2, :, cols]
            st = hl[sl, pl.ds(1, GROUPS), :, cols] + ac[sl, pl.ds(1, GROUPS), :, cols] * c
            x = rows2(src[:, :, cols] + live[1] * st).astype(BF16)
            out_buf[0, :, cols] = jnp.dot(to_tokens, x, preferred_element_type=F32).astype(BF16)

        over_heads(body)

    def scan_back(l, cols):
        z = jnp.zeros((LANES8, BLK), F32)
        b = jnp.ones((LANES8, BLK), F32)
        for t in reversed(range(GROUPS)):
            q = live[l] * dy[t, :, cols] + z
            qp[l, t, :, cols] = q
            bn[l, t, :, cols] = b
            a = st_a[l, t, :, cols]
            z = a * q
            b = a * b
        qp[l, GROUPS, :, cols] = z
        bn[l, GROUPS, :, cols] = b

    def backward(l, xref):
        def step(h, inner):
            cols = cols_of(h)
            g = gain[pl.ds(l, 1), cols]
            k8 = par[0, pl.ds(l, 1), cols]
            c, zin = ends[l, 2, :, cols], ends[3 + l, 2, :, cols]
            sums = [jnp.zeros((LANES8, BLK), F32) for _ in range(3)]
            for rows in chunks():
                q = qp[l, rows, :, cols] + bn[l, rows, :, cols] * zin
                a, r, i = st_a[l, rows, :, cols], st_r[l, rows, :, cols], st_i[l, rows, :, cols]
                sc, rs = st_s[l, rows, :, cols], st_rs[l, rows, :, cols]
                uf = (xref[rows, :, cols] * inv[l, rows] * g).astype(BF16).astype(F32)
                before = hl[l, rows, :, cols] + ac[l, rows, :, cols] * c
                iu = i * uf
                qs = q * sc
                d_log = q * a * (before - iu * a * rs)
                dr = d_log * r
                d_a = dr * k8 * (1.0 - r)
                d_x = qs * iu * (1.0 - i)
                sums[0] += jnp.sum(d_a, axis=0)
                sums[1] += jnp.sum(d_x, axis=0)
                sums[2] += jnp.sum(dr, axis=0)
                pre_a[rows] = d_a
                pre_x[rows] = d_x
                dn[rows, :, cols] = qs * i
            for k in range(3):
                gsum[l, k, :, cols] = sums[k]
            nt = (((1,), (1,)), ((), ()))
            mixed = lax.dot_general(rows2(pre_a[...]).astype(BF16), wfull[l, 0, h], nt, preferred_element_type=F32)
            mixed += lax.dot_general(rows2(pre_x[...]).astype(BF16), wfull[l, 1, h], nt, preferred_element_type=F32)
            pre_a[...] = runs3(mixed)
            total = jnp.zeros((LANES8, BLK), F32)
            out = []
            for rows in chunks():
                n = xref[rows, :, cols] * inv[l, rows]
                du = dn[rows, :, cols] + pre_a[rows]
                dnn = du * n
                total += jnp.sum(dnn, axis=0)
                dn[rows, :, cols] = du * g
                v = dnn * g
                out.append(v[..., :128] + v[..., 128:])
            gsum[l, 3, :, cols] = total
            return inner + jnp.concatenate(out, axis=0)

        inner = lax.fori_loop(0, heads, step, jnp.zeros((GROUPS, LANES8, 128), F32))
        mean = jnp.sum(inner, axis=-1, keepdims=True) * (1.0 / chans)
        inv[3] = jnp.broadcast_to(mean, inv.shape[1:])

    def through_norm(l, xref, finish):
        def body(h, cols):
            for rows in chunks():
                n = xref[rows, :, cols] * inv[l, rows]
                dy[rows, :, cols] = dy[rows, :, cols] + inv[l, rows] * (dn[rows, :, cols] - n * inv[3, rows])
            finish(cols)

        over_heads(body)

    def send_sums(l):
        scale = -8.0 * par[1, pl.ds(l, 1), :]
        for k, source in enumerate((3, 0, 1, 2)):
            v = jnp.sum(gsum[l, source], axis=0, keepdims=True)
            if k == 3:
                v = v * scale
            put_summary(eyg.at[l], k, v, 0)
        eg[l].y_start()

    def pass_sums(l):
        eg[l].y_wait()
        total = eyg[l, 0]
        for t in range(1, NY):
            total += eyg[l, t]
        exg[l, mx] = total
        eg[l].x_start()

    def put_sums(l):
        eg[l].x_wait()
        total = exg[l, 0]
        for t in range(1, NX):
            total += exg[l, t]
        for k, ref in enumerate((o_gain, o_ba, o_bx, o_rate)):
            for g in range(pieces):
                ref[l : l + 1, 128 * g : 128 * (g + 1)] = total[k, g : g + 1, :]

    half = heads // 2
    loads[0].wait()
    loads[1].wait()
    g0, g1 = gather(0), gather(1)
    step = lambda g: next(g, None)
    step(g0)
    loads[2].wait()
    store_inv(0, permuted(0, x0.at[0]))
    step(g0)
    loads[3].wait()
    store_inv(2, permuted(1, x0.at[1]))
    step(g0)
    loads[4].wait()
    permuted(2, dy)
    step(g0)
    step(g0)
    step(g1)
    step(g0)
    step(g1)
    step(g0)
    step(g0)

    forward(0, 0, x0.at[0], 0, 0, True, 0, half)
    step(g1)
    forward(0, 0, x0.at[0], 0, 0, True, half, heads)
    summarise(0, ey0.at[0])
    e0[0].y_start()
    step(g1)
    forward(0, 1, x0.at[1], 2, 2, False, 0, half)
    step(g1)
    e0[0].y_wait()
    row_total(ey0.at[0], ex0.at[0])
    e0[0].x_start()
    forward(0, 1, x0.at[1], 2, 2, False, half, heads)
    summarise(2, ey0.at[1])
    e0[1].y_start()
    step(g1)
    e0[0].x_wait()
    put_entering(0, entering(ey0.at[0], ex0.at[0]))
    store_inv(1, next_layer(x0.at[0], 0, x1.at[0]))
    step(g1)
    step(g1)
    forward(1, 0, x1.at[0], 1, 1, True, 0, half)
    e0[1].y_wait()
    row_total(ey0.at[1], ex0.at[1])
    e0[1].x_start()
    forward(1, 0, x1.at[0], 1, 1, True, half, heads)
    over_heads(lambda h, cols: scan_back(1, cols))
    summarise(1, ey1)
    summarise_back(1, ey1, 2)
    e1.y_start()
    e0[1].x_wait()
    put_entering(2, entering(ey0.at[1], ex0.at[1]))
    store_inv(2, next_layer(x0.at[1], 2, x1.at[1]))
    e1.y_wait()
    row_total(ey1, ex1)
    row_total_back(ey1, ey1, 2, ex1, 2)
    e1.x_start()
    forward(1, 1, x1.at[1], 2, 2, False, 0, heads)
    summarise(2, ey2.at[0])
    e1a.y_start()
    e1.x_wait()
    put_entering(1, entering(ey1, ex1))
    put_entering(4, entering_back(ey1, ex1, ey1, ex1, 2))
    backward(1, x1.at[0])
    through_norm(1, x1.at[0], lambda cols: scan_back(0, cols))
    summarise_back(0, ey2.at[1], 0)
    e2.y_start()
    e1a.y_wait()
    row_total(ey2.at[0], ex2.at[0])
    e1a.x_start()
    send_sums(1)
    e2.y_wait()
    row_total_back(ey0.at[0], ey2.at[1], 0, ex2.at[1], 0)
    e2.x_start()
    e1a.x_wait()
    put_entering(2, entering(ey2.at[0], ex2.at[0]))
    last_layer(x1.at[1], 2)
    send(out_buf.at[0], acts_out, (o_send, o_recv), 0, sec_next)
    e2.x_wait()
    put_entering(3, entering_back(ey0.at[0], ex0.at[0], ey2.at[1], ex2.at[1], 0))
    backward(0, x0.at[0])
    send_sums(0)
    pass_sums(1)

    def finish(cols):
        out_buf[1, :, cols] = jnp.dot(to_tokens, rows2(dy[:, :, cols]).astype(BF16), preferred_element_type=F32).astype(BF16)

    through_norm(0, x0.at[0], finish)
    send(out_buf.at[1], grad_out, (o_send, o_recv), 1, sec_prev)
    pass_sums(0)
    put_sums(1)
    put_sums(0)
    arrived(acts_out, (o_send, o_recv), 0)
    arrived(grad_out, (o_send, o_recv), 1)
    for c in sent:
        c.wait_send()


def local(acts_in, saved_in, grad_in, gate_a, gate_x, bias_a, bias_x, rate_param, norm_gain, section_layers):
    _, tokens, chans = acts_in.shape
    slots, heads = gate_a.shape[1:3]
    full = (GROUPS, LANES8, chans)
    vec = (chans // 128, 128)
    sem = pltpu.SemaphoreType.DMA
    any_spec = pl.BlockSpec(memory_space=pl.ANY)
    vmem_spec = pl.BlockSpec(memory_space=pltpu.VMEM)
    exchanges = 7 * (NX + NY - 2)
    vm = pltpu.VMEM
    outs = pl.pallas_call(
        kernel,
        out_shape=[jax.ShapeDtypeStruct((tokens, chans), BF16)] * 2
        + [jax.ShapeDtypeStruct((slots, chans), F32)] * 4,
        in_specs=[any_spec] * 5 + [vmem_spec] * 4 + [pl.BlockSpec(memory_space=pltpu.SMEM)],
        out_specs=[any_spec] * 2 + [vmem_spec] * 4,
        scratch_shapes=[
            vm((slots, NX, NY, heads, 8, BLK), BF16),
            vm((slots, NX, NY, heads, 8, BLK), BF16),
            vm((slots, 2, heads, BLK, BLK), BF16),
            vm((3, tokens, chans), BF16),
            vm((2, tokens, chans), BF16),
            vm((2, *full), F32),
            vm((2, *full), F32),
            vm((4, GROUPS, LANES8, BLK), F32),
            vm((3, GROUPS + 1, LANES8, chans), F32),
            vm((3, GROUPS + 1, LANES8, chans), F32),
            vm((slots, *full), F32),
            vm((slots, *full), F32),
            vm((slots, *full), F32),
            vm((slots, *full), F32),
            vm((slots, *full), F32),
            vm((slots, GROUPS + 1, LANES8, chans), F32),
            vm((slots, GROUPS + 1, LANES8, chans), F32),
            vm(full, F32),
            vm(full, F32),
            vm((GROUPS, LANES8, BLK), F32),
            vm((GROUPS, LANES8, BLK), F32),
            vm((5, 3, LANES8, chans), F32),
            vm((2, slots, chans), F32),
            vm((slots, 4, LANES8, chans), F32),
            vm((2, NY, 2, *vec), F32),
            vm((2, NX, 2, *vec), F32),
            vm((NY, 3, *vec), F32),
            vm((NX, 3, *vec), F32),
            vm((2, NY, 2, *vec), F32),
            vm((2, NX, 2, *vec), F32),
            vm((slots, NY, 4, *vec), F32),
            vm((slots, NX, 4, *vec), F32),
            sem((5,)),
            sem((2 * PER_LAYER,)),
            sem((2 * PER_LAYER,)),
            sem((exchanges,)),
            sem((exchanges,)),
            sem((2,)),
            sem((2,)),
        ],
        compiler_params=pltpu.CompilerParams(
            collective_id=0, has_side_effects=True, vmem_limit_bytes=60 * 1024 * 1024
        ),
    )(
        acts_in[0], saved_in[0], grad_in[0], gate_a[0], gate_x[0],
        bias_a[0], bias_x[0], rate_param[0], norm_gain[0], section_layers,
    )
    return tuple(o[None] for o in outs)


def solution(mesh):
    finer = Mesh(mesh.devices.reshape(mesh.shape["section"], NX, NY), ("section", "tm_0", "tm_1"))
    tm = ("tm_0", "tm_1")
    act = P("section", tm, None)
    gate = P("section", None, None, tm, None)
    small = P("section", None, None)
    return jax.shard_map(
        local,
        mesh=finer,
        in_specs=(act, act, act, gate, gate, small, small, small, small, P("section")),
        out_specs=(act, act, small, small, small, small),
        check_vma=False,
    )
```

time: 451 us -> 112 us (0.25)
  the two profiles are of different devices: /device:TPU:4 before, /device:TPU:48 now
where the time goes in v1:
time: 112 us; the launch traced here: 111 us
  Pallas kernels  104 us (93%)
  local copies, waits for them, and re-layouts  5.52 us (5%)
  between operations  1.31 us (1%)
    pallas_call x1, Pallas kernels, local(): pl.pallas_call(kernel, out_shape=[jax.ShapeDtypeStruct((tokens, chans), B...  104 us
    unnamed x16, local copies, waits for them, and re-layouts  5.52 us

profile of v1, /device:TPU:48, one launch (start us, length us, event | category | flops | bytes accessed | tf_op | source)
XLA Modules:
  0.0 111.1 jit_solution(16279981444336461643)
XLA Ops:
  1.3 104.3 %shard_map.145 = (bf16[128,2048]{1,0:T(8,128)(2,1)}, bf16[128,2048]{1,0:T(8,128)(2,1)}, f32[2,2048]{1,0:T(2,128)}, f32[2,2048]{1,0:T(2,128)}, f32[2,2048]{1,0:T(2,128)}, /*index=5*/f32[2,2048]{1,0:T(2,128)}) custom-call(bf16[128,2048]{1,0:T(8,128)(2,1)} %bitcast.17, bf16[128,2048]{1,0:T(8,128)(2,1)} %bitcast.18, bf16[128,2048]{1,0:T(8,128)(2,1)} %bitcast.19, ...), custom_call_target="tpu_custom_call" | custom-call | tf_op jit(solution)/shard_map/pallas_call | solution.py:594
  105.6 0.0 copy-start
  105.6 1.9 %copy.23 = bf16[1,128,2048]{2,1,0:T(8,128)(2,1)} copy(bf16[1,128,2048]{2,1,0:T(8,128)(2,1)} %bitcast.16) | data formatting | bytes 1048576
  107.5 0.0 copy-done
  107.5 0.0 copy-start.4
  107.5 0.8 copy.24
  108.3 0.0 copy-done.4
  108.3 0.0 copy-start.3
  108.3 0.6 copy.25
  108.9 0.1 copy-done.3
  109.1 0.0 copy-start.2
  109.1 0.6 copy.26
  109.7 0.1 copy-done.2
  109.8 0.0 copy-start.1
  109.8 0.6 copy.27
  110.4 0.1 copy-done.1
  110.5 0.6 copy.28
Async XLA Ops:
  105.6 2.0 %copy-start = (bf16[128,2048]{1,0:T(8,128)(2,1)S(1)}, bf16[128,2048]{1,0:T(8,128)(2,1)}, u32[]{:S(2)}) copy-start(bf16[128,2048]{1,0:T(8,128)(2,1)} %get-tuple-element.13) | copy-start | bytes 1572868
  107.5 0.8 copy-start.4
  108.3 0.7 copy-start.3
  109.1 0.7 copy-start.2
  109.8 0.7 copy-start.1

commit v2 on v1

v2 whole, which is shorter than its diff:
```python
import jax
import jax.numpy as jnp
from jax import lax
from jax.experimental import pallas as pl
from jax.experimental.pallas import tpu as pltpu
from jax.sharding import Mesh
from jax.sharding import PartitionSpec as P

MESH = pl.DeviceIdType.MESH
F32, BF16 = jnp.float32, jnp.bfloat16
EPS = 1e-06
NX, NY = 4, 8
GROUPS, LANES8 = 16, 8
BLK = 256
STEP = 4


def kernel(
    acts_hbm, saved_hbm, grad_hbm, ga_hbm, gx_hbm, bias_a, bias_x, rate_param, gain, layers,
    acts_out, grad_out, sums_out,
    w, wsrc, wfull, xin, out_buf,
    x0, x1, inv, sq, ac, hl, st_a, st_r, st_i, st_s, st_rs, qp, bn, dy, dn,
    pre_a, pre_x, ends, par, gsum,
    ey0, ey1, ey1a, ey2, eyg, exg, xsum,
    load_sem, w_send, w_recv, i_send, i_recv, e_send, e_recv, n_send, n_recv, g_send, g_recv, o_send, o_recv,
):
    s, mx, my = lax.axis_index("section"), lax.axis_index("tm_0"), lax.axis_index("tm_1")
    ns = lax.axis_size("section")
    chans = x0.shape[-1]
    heads = chans // BLK
    own = chans // NX
    mine = heads // NX
    pieces = chans // 128

    def xp(d):
        return lax.rem(mx + (d + NX), NX)

    def yp(d):
        return lax.rem(my + (d + NY), NY)

    def at_x(d):
        return (s, xp(d), my)

    def at_y(d):
        return (s, mx, yp(d))

    def section(step, d):
        return (lax.rem(s + (step + ns), ns), xp(d), my)

    def part(x):
        return pl.ds(pl.multiple_of(x * own, own), own)

    loads = [
        pltpu.make_async_copy(ga_hbm, wsrc.at[:, :, 0], load_sem.at[0]),
        pltpu.make_async_copy(gx_hbm, wsrc.at[:, :, 1], load_sem.at[1]),
        pltpu.make_async_copy(ga_hbm.at[:, mx], w.at[:, mx, my, 0], load_sem.at[2]),
        pltpu.make_async_copy(gx_hbm.at[:, mx], w.at[:, mx, my, 1], load_sem.at[3]),
    ]
    sources = (saved_hbm, acts_hbm, grad_hbm)
    loads += [
        pltpu.make_async_copy(ref.at[:, part(mx)], xin.at[k, :, part(mx)], load_sem.at[4 + k])
        for k, ref in enumerate(sources)
    ]
    for c in loads:
        c.start()

    around = [(a, b) for b in (0, 1, 7, 2, 6, 3, 5, 4) for a in (0, 1, 3, 2) if a or b]
    peers = [(s, xp(a), yp(b)) for a, b in around]
    peers += [section(step, d) for step in (1, -1) for d in range(NX)]
    barrier = pltpu.get_barrier_semaphore()
    for dev in peers:
        pl.semaphore_signal(barrier, inc=1, device_id=dev, device_id_type=MESH)
    pl.semaphore_wait(barrier, len(peers))

    sent = []

    def send(src, dst, sems, k, dev):
        c = pltpu.make_async_remote_copy(
            src_ref=src, dst_ref=dst, send_sem=sems[0].at[k], recv_sem=sems[1].at[k],
            device_id=dev, device_id_type=MESH,
        )
        c.start()
        sent.append(c)

    def arrived(slot, sems, k):
        pltpu.make_async_remote_copy(
            src_ref=slot, dst_ref=slot, send_sem=sems[0].at[k], recv_sem=sems[1].at[k],
            device_id=at_x(1), device_id_type=MESH,
        ).wait_recv()

    wsems, isems, esems = (w_send, w_recv), (i_send, i_recv), (e_send, e_recv)
    nsems, gsems, osems = (n_send, n_recv), (g_send, g_recv), (o_send, o_recv)

    def inputs_start(k):
        for d in (2, 1, 3):
            send(sources[k].at[:, part(xp(d))], xin.at[k, :, part(mx)], isems, 3 * k + d - 1, at_x(d))

    def inputs_wait(k):
        loads[4 + k].wait()
        for d in (1, 3, 2):
            arrived(xin.at[k, :, part(xp(-d))], isems, 3 * k + d - 1)

    near = [(a, b) for a, b in around if b in (0, 1, 2, NY - 1, NY - 2)]
    per_slot = len(near) + 4

    def weights_start(l):
        for n, (a, b) in enumerate(near):
            send(wsrc.at[l, xp(a)], w.at[l, mx, my], wsems, per_slot * l + n, (s, xp(a), yp(b)))

    def near_wait(l, places):
        for n, (a, b) in enumerate(near):
            if b in places:
                arrived(w.at[l, xp(-a), yp(-b)], wsems, per_slot * l + n)

    lo, hi = slice(0, NX // 2), slice(NX // 2, NX)

    def weights_pass(l):
        near_wait(l, (2, NY - 2))
        k = per_slot * l + len(near)
        for n, (xs, y, d) in enumerate(((lo, -2, 2), (hi, 2, -2), (slice(None), -2, 1), (slice(None), 2, -1))):
            ref = w.at[l, xs, yp(y)]
            send(ref, ref, wsems, k + n, at_y(d))

    def weights_wait(l):
        near_wait(l, (0, 1, NY - 1))
        k = per_slot * l + len(near)
        for n, (xs, y) in enumerate(((lo, 4), (hi, 4), (slice(None), -3), (slice(None), 3))):
            arrived(w.at[l, xs, yp(y)], wsems, k + n)

    class Exchange:
        def __init__(self, number, yb, sems=esems):
            self.base, self.yb, self.sems = number * (NY - 1), yb, sems

        def start(self):
            for d in (4, 3, 5, 2, 6, 1, 7):
                send(self.yb.at[my], self.yb.at[my], self.sems, self.base + d - 1, at_y(d))

        def wait(self):
            for d in range(1, NY):
                arrived(self.yb.at[yp(-d)], self.sems, self.base + d - 1)

    e0 = [Exchange(k, ey0.at[k]) for k in (0, 1)]
    e1 = Exchange(2, ey1)
    e1a = Exchange(3, ey1a)
    e2 = Exchange(4, ey2)
    eg = [Exchange(5 + l, eyg.at[l]) for l in (0, 1)]

    y = jnp.exp(rate_param[...])
    rate = y * (1.0 + y * (-1.0 / 2 + y * (1.0 / 3 + y * (-1.0 / 4 + y * (1.0 / 5 + y * (-1.0 / 6))))))
    par[0] = -8.0 * rate
    par[1] = y / (1.0 + y)
    live = [jnp.minimum(jnp.maximum(layers[0] - l, 0), 1).astype(F32) for l in (0, 1)]

    tok = lax.broadcasted_iota(jnp.int32, (128, 128), 1)
    row = lax.broadcasted_iota(jnp.int32, (128, 128), 0)
    to_runs = (tok == (row % LANES8) * GROUPS + row // LANES8).astype(F32).astype(BF16)
    to_tokens = (row == (tok % LANES8) * GROUPS + tok // LANES8).astype(F32).astype(BF16)
    sub = lax.broadcasted_iota(jnp.int32, (LANES8, chans), 0)
    sub16 = lax.broadcasted_iota(jnp.int32, (pieces, 128), 0)

    def cols_of(h):
        return pl.ds(pl.multiple_of(h * BLK, BLK), BLK)

    def over_heads(body, lo=0, hi=None):
        def step(h, _):
            body(h, cols_of(h))
            return 0

        lax.fori_loop(lo, heads if hi is None else hi, step, 0)

    def chunks():
        return [pl.ds(c * STEP, STEP) for c in range(GROUPS // STEP)]

    def runs3(v):
        return v.reshape(GROUPS, LANES8, v.shape[-1])

    def rows2(v):
        return v.reshape(GROUPS * LANES8, v.shape[-1])

    def squares(x):
        sq = x * x
        return sq[..., :128] + sq[..., 128:]

    def params_of(v):
        return pl.ds(pl.multiple_of((mx * mine + lax.rem(v, mine)) * BLK, BLK), BLK)

    def share(n):
        tile = jnp.zeros((128, 128), F32)
        for b in range(NX):
            both = sq[mine * b]
            for k in range(1, mine):
                both += sq[mine * b + k]
            tile = jnp.where(tok == b, jnp.sum(rows2(both), axis=1, keepdims=True), tile)
        xsum[n, mx] = tile.T[:LANES8]
        for d in (2, 1, 3):
            send(xsum.at[n, mx], xsum.at[n, mx], nsems, 3 * n + d - 1, at_x(d))

    def shared(n):
        for d in (1, 3, 2):
            arrived(xsum.at[n, xp(-d)], nsems, 3 * n + d - 1)
        total = xsum[n, 0]
        for x in range(1, NX):
            total += xsum[n, x]
        return total * (1.0 / chans)

    def put_rows(slot, tile):
        turned = tile.T
        for b in range(NX):
            inv[slot, b] = runs3(jnp.broadcast_to(turned[:, b : b + 1], (128, BLK)))

    def put_inv(slot, n):
        put_rows(slot, lax.rsqrt(shared(n) + EPS))

    def permuted(k, dst, summed):
        def body(v, cols):
            x = runs3(jnp.dot(to_runs, xin[k, :, cols], preferred_element_type=F32))
            dst[:, :, cols] = x
            if summed:
                sq[v] = squares(x)

        over_heads(body)

    def assemble(l):
        for g in (0, 1):
            for k in range(mine):
                wfull[l, g, k] = w[l, :, :, g, k].astype(F32).reshape(BLK, BLK).astype(BF16)

    def sigmoid(v):
        return 1.0 / (1.0 + jnp.exp(-v))

    def forward(l, stream, xref, kk, sl):
        def body(v, cols):
            pc, h, b = params_of(v), lax.rem(v, mine), v // mine
            g = gain[pl.ds(l, 1), pc]
            ba, bx = bias_a[pl.ds(l, 1), pc], bias_x[pl.ds(l, 1), pc]
            k8 = par[0, pl.ds(l, 1), pc]
            w_a, w_x = wfull[l, 0, h], wfull[l, 1, h]
            u = rows2(xref[:, :, cols] * inv[kk, b] * g).astype(BF16)
            pre_a[...] = runs3(jnp.dot(u, w_a, preferred_element_type=F32))
            pre_x[...] = runs3(jnp.dot(u, w_x, preferred_element_type=F32))
            cum_a = jnp.ones((LANES8, BLK), F32)
            cum_h = jnp.zeros((LANES8, BLK), F32)
            for c, rows in enumerate(chunks()):
                uf = (xref[rows, :, cols] * inv[kk, b, rows] * g).astype(BF16).astype(F32)
                r = sigmoid(pre_a[rows] + ba)
                i = sigmoid(pre_x[rows] + bx)
                log_a = r * k8
                a = jnp.exp(log_a)
                z = log_a * 2.0
                p = 1.0 / 120 + z * (1.0 / 720)
                p = 1.0 / 24 + z * p
                p = 1.0 / 6 + z * p
                p = 0.5 + z * p
                p = 1.0 + z * p
                sc2 = -(z * p)
                rs = lax.rsqrt(jnp.maximum(sc2, 1e-36))
                sc = sc2 * rs
                up = sc * i * uf
                if stream == 0:
                    st_a[l, rows, :, cols] = a
                    st_r[l, rows, :, cols] = r
                    st_i[l, rows, :, cols] = i
                    st_s[l, rows, :, cols] = sc
                    st_rs[l, rows, :, cols] = rs
                for t in range(STEP):
                    cum_a = cum_a * a[t]
                    cum_h = a[t] * cum_h + up[t]
                    ac[sl, c * STEP + t + 1, :, cols] = cum_a
                    hl[sl, c * STEP + t + 1, :, cols] = cum_h
            ac[sl, 0, :, cols] = jnp.ones((LANES8, BLK), F32)
            hl[sl, 0, :, cols] = jnp.zeros((LANES8, BLK), F32)

        over_heads(body)

    def shifted(v, n, fill):
        if n > 0:
            return jnp.where(sub >= n, pltpu.roll(v, n, 0), fill)
        return jnp.where(sub < LANES8 + n, pltpu.roll(v, LANES8 + n, 0), fill)

    def joined(a, h, sign):
        for n in (1, 2, 4):
            h = a * shifted(h, sign * n, 0.0) + h
            a = a * shifted(a, sign * n, 1.0)
        return a, h

    def put_summary(dst, k, full, at):
        for g in range(pieces):
            dst[my, k, g : g + 1, :] = full[at : at + 1, 128 * g : 128 * (g + 1)]

    def summarise(sl, dst):
        a, h = joined(ac[sl, GROUPS], hl[sl, GROUPS], 1)
        ends[sl, 0] = shifted(a, 1, 1.0)
        ends[sl, 1] = shifted(h, 1, 0.0)
        put_summary(dst, 0, a, LANES8 - 1)
        put_summary(dst, 1, h, LANES8 - 1)

    def summarise_back(l, dst, k):
        a, z = joined(bn[l, GROUPS], qp[l, GROUPS], -1)
        ends[3 + l, 0] = shifted(a, -1, 1.0)
        ends[3 + l, 1] = shifted(z, -1, 0.0)
        put_summary(dst, k, z, 0)

    def entering(yb):
        a, h = yb[0, 0], yb[0, 1]
        for t in range(1, NY):
            h = yb[t, 0] * h + yb[t, 1]
            a = yb[t, 0] * a
        per = pieces // NX
        state = jnp.zeros((pieces, 128), F32)
        for _ in range(NX - 1):
            state = jnp.where(sub16 >= per, pltpu.roll(a * state + h, per, 0), 0.0)
        for t in range(NY - 1):
            state = jnp.where(t < my, yb[t, 0] * state + yb[t, 1], state)
        return state

    def entering_back(ya, yz, kz):
        z = yz[NY - 1, kz]
        a = ya[NY - 1, 0]
        for t in reversed(range(NY - 1)):
            z = ya[t, 0] * z + yz[t, kz]
            a = ya[t, 0] * a
        per = pieces // NX
        state = jnp.zeros((pieces, 128), F32)
        for _ in range(NX - 1):
            state = jnp.where(sub16 < pieces - per, pltpu.roll(a * state + z, pieces - per, 0), 0.0)
        for t in reversed(range(1, NY)):
            state = jnp.where(t > my, ya[t, 0] * state + yz[t, kz], state)
        return state

    def put_entering(k, h):
        for g in range(pieces):
            c = slice(128 * g, 128 * (g + 1))
            ends[k, 2, :, c] = ends[k, 1, :, c] + ends[k, 0, :, c] * h[g : g + 1]

    def next_layer(src, sl, dst):
        def body(v, cols):
            c = ends[sl, 2, :, cols]
            for k in range(GROUPS // STEP):
                rows, later = pl.ds(k * STEP, STEP), pl.ds(k * STEP + 1, STEP)
                st = hl[sl, later, :, cols] + ac[sl, later, :, cols] * c
                x = (src[rows, :, cols] + live[0] * st).astype(BF16).astype(F32)
                dst[rows, :, cols] = x
                sq[v, rows] = squares(x)

        over_heads(body)

    def last_layer(src, sl):
        def body(h, cols):
            c = ends[sl, 2, :, cols]
            st = hl[sl, pl.ds(1, GROUPS), :, cols] + ac[sl, pl.ds(1, GROUPS), :, cols] * c
            x = rows2(src[:, :, cols] + live[1] * st).astype(BF16)
            out_buf[0, :, cols] = jnp.dot(to_tokens, x, preferred_element_type=F32).astype(BF16)

        over_heads(body)

    def scan_back(l, cols):
        z = jnp.zeros((LANES8, BLK), F32)
        b = jnp.ones((LANES8, BLK), F32)
        for t in reversed(range(GROUPS)):
            q = live[l] * dy[t, :, cols] + z
            qp[l, t, :, cols] = q
            bn[l, t, :, cols] = b
            a = st_a[l, t, :, cols]
            z = a * q
            b = a * b
        qp[l, GROUPS, :, cols] = z
        bn[l, GROUPS, :, cols] = b

    def backward(l, xref):
        def body(v, cols):
            pc, h, b = params_of(v), lax.rem(v, mine), v // mine
            g = gain[pl.ds(l, 1), pc]
            k8 = par[0, pl.ds(l, 1), pc]
            c, zin = ends[l, 2, :, cols], ends[3 + l, 2, :, cols]
            sums = [jnp.zeros((LANES8, BLK), F32) for _ in range(3)]
            for rows in chunks():
                q = qp[l, rows, :, cols] + bn[l, rows, :, cols] * zin
                a, r, i = st_a[l, rows, :, cols], st_r[l, rows, :, cols], st_i[l, rows, :, cols]
                sc, rs = st_s[l, rows, :, cols], st_rs[l, rows, :, cols]
                uf = (xref[rows, :, cols] * inv[l, b, rows] * g).astype(BF16).astype(F32)
                before = hl[l, rows, :, cols] + ac[l, rows, :, cols] * c
                iu = i * uf
                qs = q * sc
                d_log = q * a * (before - iu * a * rs)
                dr = d_log * r
                d_a = dr * k8 * (1.0 - r)
                d_x = qs * iu * (1.0 - i)
                sums[0] += jnp.sum(d_a, axis=0)
                sums[1] += jnp.sum(d_x, axis=0)
                sums[2] += jnp.sum(dr, axis=0)
                pre_a[rows] = d_a
                pre_x[rows] = d_x
                dn[rows, :, cols] = qs * i
            for k in range(3):
                gsum[l, k, :, cols] = sums[k]
            nt = (((1,), (1,)), ((), ()))
            mixed = lax.dot_general(rows2(pre_a[...]).astype(BF16), wfull[l, 0, h], nt, preferred_element_type=F32)
            mixed += lax.dot_general(rows2(pre_x[...]).astype(BF16), wfull[l, 1, h], nt, preferred_element_type=F32)
            pre_a[...] = runs3(mixed)
            total = jnp.zeros((LANES8, BLK), F32)
            for rows in chunks():
                n = xref[rows, :, cols] * inv[l, b, rows]
                du = dn[rows, :, cols] + pre_a[rows]
                dnn = du * n
                total += jnp.sum(dnn, axis=0)
                dn[rows, :, cols] = du * g
                t = dnn * g
                sq[v, rows] = t[..., :128] + t[..., 128:]
            gsum[l, 3, :, cols] = total

        over_heads(body)

    def through_norm(l, xref, finish, lo=0, hi=None):
        def body(v, cols):
            b = v // mine
            for rows in chunks():
                n = xref[rows, :, cols] * inv[l, b, rows]
                dy[rows, :, cols] = dy[rows, :, cols] + inv[l, b, rows] * (dn[rows, :, cols] - n * inv[3, b, rows])
            finish(cols)

        over_heads(body, lo, hi)

    def send_sums(l):
        for k, source in enumerate((3, 0, 1, 2)):
            v = gsum[l, source, :, :own]
            for b in range(1, NX):
                v += gsum[l, source, :, b * own : (b + 1) * own]
            v = jnp.sum(v, axis=0, keepdims=True)
            if k == 3:
                v = v * (-8.0 * par[1, pl.ds(l, 1), part(mx)])
            for g in range(own // 128):
                at = k * (own // 128) + g
                eyg[l, my, at : at + 1, :] = v[:, 128 * g : 128 * (g + 1)]
        eg[l].start()

    def pass_sums(l):
        eg[l].wait()
        total = eyg[l, 0]
        for t in range(1, NY):
            total += eyg[l, t]
        exg[l, mx] = total
        for d in (2, 1, 3):
            send(exg.at[l, mx], exg.at[l, mx], gsems, 3 * l + d - 1, at_x(d))

    def put_sums(l):
        for d in (1, 3, 2):
            arrived(exg.at[l, xp(-d)], gsems, 3 * l + d - 1)
        sums_out[l] = exg[l]

    def deliver(k, result, step, d):
        send(out_buf.at[k, :, part(xp(d))], result.at[:, part(mx)], osems, NX * k + d, section(step, d))

    def delivered(k, result, d):
        arrived(result.at[:, part(xp(-d))], osems, NX * k + d)

    loads[0].wait()
    loads[1].wait()
    inputs_start(0)
    weights_start(0)
    inputs_wait(0)
    permuted(0, x0.at[0], True)
    share(0)
    weights_pass(0)
    weights_start(1)
    inputs_start(1)
    put_inv(0, 0)
    loads[2].wait()
    loads[3].wait()
    weights_wait(0)
    assemble(0)
    forward(0, 0, x0.at[0], 0, 0)
    summarise(0, ey0.at[0])
    e0[0].start()
    inputs_wait(1)
    permuted(1, x0.at[1], True)
    share(1)
    weights_pass(1)
    inputs_start(2)
    put_inv(2, 1)
    forward(0, 1, x0.at[1], 2, 2)
    e0[0].wait()
    put_entering(0, entering(ey0.at[0]))
    next_layer(x0.at[0], 0, x1.at[0])
    share(2)
    summarise(2, ey0.at[1])
    e0[1].start()
    inputs_wait(2)
    permuted(2, dy, False)
    weights_wait(1)
    assemble(1)
    put_inv(1, 2)
    forward(1, 0, x1.at[0], 1, 1)
    over_heads(lambda v, cols: scan_back(1, cols))
    summarise(1, ey1)
    summarise_back(1, ey1, 2)
    e1.start()
    e0[1].wait()
    put_entering(2, entering(ey0.at[1]))
    next_layer(x0.at[1], 2, x1.at[1])
    share(3)
    put_inv(2, 3)
    e1.wait()
    put_entering(1, entering(ey1))
    put_entering(4, entering_back(ey1, ey1, 2))
    backward(1, x1.at[0])
    share(4)
    forward(1, 1, x1.at[1], 2, 2)
    put_rows(3, shared(4))
    through_norm(1, x1.at[0], lambda cols: scan_back(0, cols))
    summarise_back(0, ey2, 0)
    e2.start()
    summarise(2, ey1a)
    e1a.start()
    send_sums(1)
    e2.wait()
    put_entering(3, entering_back(ey0.at[0], ey2, 0))
    backward(0, x0.at[0])
    share(5)
    send_sums(0)
    e1a.wait()
    put_entering(2, entering(ey1a))
    last_layer(x1.at[1], 2)
    for d in (2, 1, 3, 0):
        deliver(0, acts_out, 1, d)
    put_rows(3, shared(5))

    def finish(cols):
        out_buf[1, :, cols] = jnp.dot(to_tokens, rows2(dy[:, :, cols]).astype(BF16), preferred_element_type=F32).astype(BF16)

    for d in (2, 1, 3, 0):
        through_norm(0, x0.at[0], finish, mine * xp(d), mine * xp(d) + mine)
        deliver(1, grad_out, -1, d)
    pass_sums(1)
    pass_sums(0)
    put_sums(1)
    put_sums(0)
    for d in range(NX):
        delivered(0, acts_out, d)
        delivered(1, grad_out, d)
    for c in sent:
        c.wait_send()


def hand_over(acts, grad, sums, acts_out, grad_out, o_gain, o_ba, o_bx, o_rate):
    acts_out[...] = acts[...]
    grad_out[...] = grad[...]
    per = sums.shape[2] // 4
    for k, ref in enumerate((o_gain, o_ba, o_bx, o_rate)):
        for g in range(ref.shape[-1] // 128):
            ref[:, 128 * g : 128 * (g + 1)] = sums[:, g // per, k * per + g % per, :]


def local(acts_in, saved_in, grad_in, gate_a, gate_x, bias_a, bias_x, rate_param, norm_gain, section_layers):
    _, tokens, chans = acts_in.shape
    slots, heads = gate_a.shape[1:3]
    full = (GROUPS, LANES8, chans)
    vec = (chans // 128, 128)
    sem = pltpu.SemaphoreType.DMA
    any_spec = pl.BlockSpec(memory_space=pl.ANY)
    vmem_spec = pl.BlockSpec(memory_space=pltpu.VMEM)
    mine = heads // NX
    vm = pltpu.VMEM
    outs = pl.pallas_call(
        kernel,
        out_shape=[jax.ShapeDtypeStruct((tokens, chans), BF16)] * 2
        + [jax.ShapeDtypeStruct((slots, NX, *vec), F32)],
        in_specs=[any_spec] * 5 + [vmem_spec] * 4 + [pl.BlockSpec(memory_space=pltpu.SMEM)],
        out_specs=[any_spec] * 2 + [vmem_spec],
        scratch_shapes=[
            vm((slots, NX, NY, 2, mine, 8, BLK), BF16),
            vm((slots, NX, 2, mine, 8, BLK), BF16),
            vm((slots, 2, mine, BLK, BLK), BF16),
            vm((3, tokens, chans), BF16),
            vm((2, tokens, chans), BF16),
            vm((2, *full), F32),
            vm((2, *full), F32),
            vm((4, NX, GROUPS, LANES8, BLK), F32),
            vm((heads, GROUPS, LANES8, 128), F32),
            vm((3, GROUPS + 1, LANES8, chans), F32),
            vm((3, GROUPS + 1, LANES8, chans), F32),
            vm((slots, *full), F32),
            vm((slots, *full), F32),
            vm((slots, *full), F32),
            vm((slots, *full), F32),
            vm((slots, *full), F32),
            vm((slots, GROUPS + 1, LANES8, chans), F32),
            vm((slots, GROUPS + 1, LANES8, chans), F32),
            vm(full, F32),
            vm(full, F32),
            vm((GROUPS, LANES8, BLK), F32),
            vm((GROUPS, LANES8, BLK), F32),
            vm((5, 3, LANES8, chans), F32),
            vm((2, slots, chans), F32),
            vm((slots, 4, LANES8, chans), F32),
            vm((2, NY, 2, *vec), F32),
            vm((NY, 3, *vec), F32),
            vm((NY, 2, *vec), F32),
            vm((NY, 1, *vec), F32),
            vm((slots, NY, *vec), F32),
            vm((slots, NX, *vec), F32),
            vm((6, NX, LANES8, 128), F32),
            sem((7,)),
            *[sem((slots * (5 * NX - 1 + 4),))] * 2,
            *[sem((3 * (NX - 1),))] * 2,
            *[sem((7 * (NY - 1),))] * 2,
            *[sem((6 * (NX - 1),))] * 2,
            *[sem((slots * (NX - 1),))] * 2,
            *[sem((2 * NX,))] * 2,
        ],
        compiler_params=pltpu.CompilerParams(
            collective_id=0, has_side_effects=True, vmem_limit_bytes=60 * 1024 * 1024
        ),
    )(
        acts_in[0], saved_in[0], grad_in[0],
        *(g[0].reshape(slots, NX, mine, 8, BLK) for g in (gate_a, gate_x)),
        bias_a[0], bias_x[0], rate_param[0], norm_gain[0], section_layers,
    )
    outs = pl.pallas_call(
        hand_over,
        out_shape=[jax.ShapeDtypeStruct((tokens, chans), BF16)] * 2
        + [jax.ShapeDtypeStruct((slots, chans), F32)] * 4,
        in_specs=[vmem_spec] * 3,
        out_specs=[vmem_spec] * 6,
    )(*outs)
    return tuple(o[None] for o in outs)


def solution(mesh):
    finer = Mesh(mesh.devices.reshape(mesh.shape["section"], NX, NY), ("section", "tm_0", "tm_1"))
    tm = ("tm_0", "tm_1")
    act = P("section", tm, None)
    gate = P("section", None, None, tm, None)
    small = P("section", None, None)
    return jax.shard_map(
        local,
        mesh=finer,
        in_specs=(act, act, act, gate, gate, small, small, small, small, P("section")),
        out_specs=(act, act, small, small, small, small),
        check_vma=False,
    )
```

time: 112 us -> 94.3 us (0.84)
  the two profiles are of different devices: /device:TPU:48 before, /device:TPU:1 now
where the time goes in v2:
time: 94.3 us; the launch traced here: 93.3 us
  Pallas kernels  92 us (98%)
  between operations  1.29 us (1%)
    pallas_call x1, Pallas kernels, local(): pl.pallas_call(kernel, out_shape=[jax.ShapeDtypeStruct((tokens, chans), B...  89.8 us
    pallas_call x1, Pallas kernels, local(): pl.pallas_call(hand_over, out_shape=[jax.ShapeDtypeStruct((tokens, chans)...  2.23 us

profile of v2, /device:TPU:1, one launch (start us, length us, event | category | flops | bytes accessed | tf_op | source)
XLA Modules:
  0.0 93.3 jit_solution(17506022443029401334)
XLA Ops:
  1.3 89.8 %shard_map.145 = (bf16[128,2048]{1,0:T(8,128)(2,1)}, bf16[128,2048]{1,0:T(8,128)(2,1)}, f32[2,4,16,128]{3,2,1,0:T(8,128)}) custom-call(bf16[128,2048]{1,0:T(8,128)(2,1)} %bitcast.15, bf16[128,2048]{1,0:T(8,128)(2,1)} %bitcast.16, bf16[128,2048]{1,0:T(8,128)(2,1)} %bitcast.17, bf16[2,4,2,8,256]{4,3,2,1,0:T(8,128)(2,1)} %bitcast.18, ...), custom_call_target="tpu_custom_call" | custom-call | tf_op jit(solution)/shard_map/pallas_call | solution.py:563
  91.1 2.2 %shard_map.146 = (bf16[128,2048]{1,0:T(8,128)(2,1)}, bf16[128,2048]{1,0:T(8,128)(2,1)}, f32[2,2048]{1,0:T(2,128)}, f32[2,2048]{1,0:T(2,128)}, f32[2,2048]{1,0:T(2,128)}, /*index=5*/f32[2,2048]{1,0:T(2,128)}) custom-call(bf16[128,2048]{1,0:T(8,128)(2,1)} %get-tuple-element.15.acts, bf16[128,2048]{1,0:T(8,128)(2,1)} %get-tuple-element.16.grad, ...), custom_call_target="tpu_custom_call" | custom-call | tf_op jit(solution)/shard_map/pallas_call | solution.py:618

commit v3 on v2

--- a/solution.py
+++ b/solution.py
@@ -21,7 +21,7 @@
     w, wsrc, wfull, xin, out_buf,
     x0, x1, inv, sq, ac, hl, st_a, st_r, st_i, st_s, st_rs, qp, bn, dy, dn,
     pre_a, pre_x, ends, par, gsum,
-    ey0, ey1, ey1a, ey2, eyg, exg, xsum,
+    lines, ey0, ey1, ey1a, ey2, eyg, exg, xsum,
     load_sem, w_send, w_recv, i_send, i_recv, e_send, e_recv, n_send, n_recv, g_send, g_recv, o_send, o_recv,
 ):
     s, mx, my = lax.axis_index("section"), lax.axis_index("tm_0"), lax.axis_index("tm_1")
@@ -181,8 +181,16 @@
         sq = x * x
         return sq[..., :128] + sq[..., 128:]
 
-    def params_of(v):
-        return pl.ds(pl.multiple_of((mx * mine + lax.rem(v, mine)) * BLK, BLK), BLK)
+    def params_of(h):
+        return pl.ds(pl.multiple_of((mx * mine + h) * BLK, BLK), BLK)
+
+    def over_blocks(body):
+        def step(b, _):
+            for h in range(mine):
+                body(b * mine + h, cols_of(b * mine + h), h, b)
+            return 0
+
+        lax.fori_loop(0, NX, step, 0)
 
     def share(n):
         tile = jnp.zeros((128, 128), F32)
@@ -229,21 +237,21 @@
         return 1.0 / (1.0 + jnp.exp(-v))
 
     def forward(l, stream, xref, kk, sl):
-        def body(v, cols):
-            pc, h, b = params_of(v), lax.rem(v, mine), v // mine
+        def body(v, cols, h, b):
+            pc = params_of(h)
             g = gain[pl.ds(l, 1), pc]
             ba, bx = bias_a[pl.ds(l, 1), pc], bias_x[pl.ds(l, 1), pc]
             k8 = par[0, pl.ds(l, 1), pc]
             w_a, w_x = wfull[l, 0, h], wfull[l, 1, h]
             u = rows2(xref[:, :, cols] * inv[kk, b] * g).astype(BF16)
-            pre_a[...] = runs3(jnp.dot(u, w_a, preferred_element_type=F32))
-            pre_x[...] = runs3(jnp.dot(u, w_x, preferred_element_type=F32))
+            pre_a[h] = runs3(jnp.dot(u, w_a, preferred_element_type=F32))
+            pre_x[h] = runs3(jnp.dot(u, w_x, preferred_element_type=F32))
             cum_a = jnp.ones((LANES8, BLK), F32)
             cum_h = jnp.zeros((LANES8, BLK), F32)
             for c, rows in enumerate(chunks()):
                 uf = (xref[rows, :, cols] * inv[kk, b, rows] * g).astype(BF16).astype(F32)
-                r = sigmoid(pre_a[rows] + ba)
-                i = sigmoid(pre_x[rows] + bx)
+                r = sigmoid(pre_a[h, rows] + ba)
+                i = sigmoid(pre_x[h, rows] + bx)
                 log_a = r * k8
                 a = jnp.exp(log_a)
                 z = log_a * 2.0
@@ -270,7 +278,7 @@
             ac[sl, 0, :, cols] = jnp.ones((LANES8, BLK), F32)
             hl[sl, 0, :, cols] = jnp.zeros((LANES8, BLK), F32)
 
-        over_heads(body)
+        over_blocks(body)
 
     def shifted(v, n, fill):
         if n > 0:
@@ -285,13 +293,14 @@
 
     def put_summary(dst, k, full, at):
         for g in range(pieces):
-            dst[my, k, g : g + 1, :] = full[at : at + 1, 128 * g : 128 * (g + 1)]
+            lines[k, g : g + 1, :] = full[at : at + 1, 128 * g : 128 * (g + 1)]
+        dst[my, k] = lines[k].astype(BF16)
 
     def summarise(sl, dst):
         a, h = joined(ac[sl, GROUPS], hl[sl, GROUPS], 1)
         ends[sl, 0] = shifted(a, 1, 1.0)
         ends[sl, 1] = shifted(h, 1, 0.0)
-        put_summary(dst, 0, a, LANES8 - 1)
+        put_summary(dst, 0, jnp.log(a), LANES8 - 1)
         put_summary(dst, 1, h, LANES8 - 1)
 
     def summarise_back(l, dst, k):
@@ -300,31 +309,37 @@
         ends[3 + l, 1] = shifted(z, -1, 0.0)
         put_summary(dst, k, z, 0)
 
+    def read(y, k):
+        vals = [y[t, k].astype(F32) for t in range(NY)]
+        return [jnp.exp(v) for v in vals] if k == 0 else vals
+
     def entering(yb):
-        a, h = yb[0, 0], yb[0, 1]
+        ya, yh = read(yb, 0), read(yb, 1)
+        a, h = ya[0], yh[0]
         for t in range(1, NY):
-            h = yb[t, 0] * h + yb[t, 1]
-            a = yb[t, 0] * a
+            h = ya[t] * h + yh[t]
+            a = ya[t] * a
         per = pieces // NX
         state = jnp.zeros((pieces, 128), F32)
         for _ in range(NX - 1):
             state = jnp.where(sub16 >= per, pltpu.roll(a * state + h, per, 0), 0.0)
         for t in range(NY - 1):
-            state = jnp.where(t < my, yb[t, 0] * state + yb[t, 1], state)
+            state = jnp.where(t < my, ya[t] * state + yh[t], state)
         return state
 
-    def entering_back(ya, yz, kz):
-        z = yz[NY - 1, kz]
-        a = ya[NY - 1, 0]
+    def entering_back(first, second, kz):
+        ya = read(first, 0)
+        yz = [second[t, kz].astype(F32) for t in range(NY)]
+        a, z = ya[NY - 1], yz[NY - 1]
         for t in reversed(range(NY - 1)):
-            z = ya[t, 0] * z + yz[t, kz]
-            a = ya[t, 0] * a
+            z = ya[t] * z + yz[t]
+            a = ya[t] * a
         per = pieces // NX
         state = jnp.zeros((pieces, 128), F32)
         for _ in range(NX - 1):
             state = jnp.where(sub16 < pieces - per, pltpu.roll(a * state + z, pieces - per, 0), 0.0)
         for t in reversed(range(1, NY)):
-            state = jnp.where(t > my, ya[t, 0] * state + yz[t, kz], state)
+            state = jnp.where(t > my, ya[t] * state + yz[t], state)
         return state
 
     def put_entering(k, h):
@@ -367,8 +382,8 @@
         bn[l, GROUPS, :, cols] = b
 
     def backward(l, xref):
-        def body(v, cols):
-            pc, h, b = params_of(v), lax.rem(v, mine), v // mine
+        def body(v, cols, h, b):
+            pc = params_of(h)
             g = gain[pl.ds(l, 1), pc]
             k8 = par[0, pl.ds(l, 1), pc]
             c, zin = ends[l, 2, :, cols], ends[3 + l, 2, :, cols]
@@ -388,19 +403,19 @@
                 sums[0] += jnp.sum(d_a, axis=0)
                 sums[1] += jnp.sum(d_x, axis=0)
                 sums[2] += jnp.sum(dr, axis=0)
-                pre_a[rows] = d_a
-                pre_x[rows] = d_x
+                pre_a[h, rows] = d_a
+                pre_x[h, rows] = d_x
                 dn[rows, :, cols] = qs * i
             for k in range(3):
                 gsum[l, k, :, cols] = sums[k]
             nt = (((1,), (1,)), ((), ()))
-            mixed = lax.dot_general(rows2(pre_a[...]).astype(BF16), wfull[l, 0, h], nt, preferred_element_type=F32)
-            mixed += lax.dot_general(rows2(pre_x[...]).astype(BF16), wfull[l, 1, h], nt, preferred_element_type=F32)
-            pre_a[...] = runs3(mixed)
+            mixed = lax.dot_general(rows2(pre_a[h]).astype(BF16), wfull[l, 0, h], nt, preferred_element_type=F32)
+            mixed += lax.dot_general(rows2(pre_x[h]).astype(BF16), wfull[l, 1, h], nt, preferred_element_type=F32)
+            pre_a[h] = runs3(mixed)
             total = jnp.zeros((LANES8, BLK), F32)
             for rows in chunks():
                 n = xref[rows, :, cols] * inv[l, b, rows]
-                du = dn[rows, :, cols] + pre_a[rows]
+                du = dn[rows, :, cols] + pre_a[h, rows]
                 dnn = du * n
                 total += jnp.sum(dnn, axis=0)
                 dn[rows, :, cols] = du * g
@@ -408,7 +423,7 @@
                 sq[v, rows] = t[..., :128] + t[..., 128:]
             gsum[l, 3, :, cols] = total
 
-        over_heads(body)
+        over_blocks(body)
 
     def through_norm(l, xref, finish, lo=0, hi=None):
         def body(v, cols):
@@ -587,15 +602,16 @@
             vm((slots, GROUPS + 1, LANES8, chans), F32),
             vm(full, F32),
             vm(full, F32),
-            vm((GROUPS, LANES8, BLK), F32),
-            vm((GROUPS, LANES8, BLK), F32),
+            vm((mine, GROUPS, LANES8, BLK), F32),
+            vm((mine, GROUPS, LANES8, BLK), F32),
             vm((5, 3, LANES8, chans), F32),
             vm((2, slots, chans), F32),
             vm((slots, 4, LANES8, chans), F32),
-            vm((2, NY, 2, *vec), F32),
-            vm((NY, 3, *vec), F32),
-            vm((NY, 2, *vec), F32),
-            vm((NY, 1, *vec), F32),
+            vm((3, *vec), F32),
+            vm((2, NY, 2, *vec), BF16),
+            vm((NY, 3, *vec), BF16),
+            vm((NY, 2, *vec), BF16),
+            vm((NY, 1, *vec), BF16),
             vm((slots, NY, *vec), F32),
             vm((slots, NX, *vec), F32),
             vm((6, NX, LANES8, 128), F32),

time: 94.3 us -> 91.6 us (0.971)
  Pallas kernels: 92 us -> 90.1 us
    pallas_call x1, Pallas kernels: 89.8 us -> 87.8 us  [local(): pl.pallas_call(kernel, out_shape=[jax.ShapeDtypeStruct((tokens, chans), B...]
where the time goes in v3:
time: 91.6 us; the launch traced here: 91.4 us
  Pallas kernels  90.1 us (98%)
  between operations  1.29 us (1%)
    pallas_call x1, Pallas kernels, local(): pl.pallas_call(kernel, out_shape=[jax.ShapeDtypeStruct((tokens, chans), B...  87.8 us
    pallas_call x1, Pallas kernels, local(): pl.pallas_call(hand_over, out_shape=[jax.ShapeDtypeStruct((tokens, chans)...  2.23 us

profile of v3, /device:TPU:1, one launch (start us, length us, event | category | flops | bytes accessed | tf_op | source)
XLA Modules:
  0.0 91.4 jit_solution(468040595848134788)
XLA Ops:
  1.3 87.8 %shard_map.145 = (bf16[128,2048]{1,0:T(8,128)(2,1)}, bf16[128,2048]{1,0:T(8,128)(2,1)}, f32[2,4,16,128]{3,2,1,0:T(8,128)}) custom-call(bf16[128,2048]{1,0:T(8,128)(2,1)} %bitcast.15, bf16[128,2048]{1,0:T(8,128)(2,1)} %bitcast.16, bf16[128,2048]{1,0:T(8,128)(2,1)} %bitcast.17, bf16[2,4,2,8,256]{4,3,2,1,0:T(8,128)(2,1)} %bitcast.18, ...), custom_call_target="tpu_custom_call" | custom-call | tf_op jit(solution)/shard_map/pallas_call | solution.py:578
  89.1 2.2 %shard_map.146 = (bf16[128,2048]{1,0:T(8,128)(2,1)}, bf16[128,2048]{1,0:T(8,128)(2,1)}, f32[2,2048]{1,0:T(2,128)}, f32[2,2048]{1,0:T(2,128)}, f32[2,2048]{1,0:T(2,128)}, /*index=5*/f32[2,2048]{1,0:T(2,128)}) custom-call(bf16[128,2048]{1,0:T(8,128)(2,1)} %get-tuple-element.15.acts, bf16[128,2048]{1,0:T(8,128)(2,1)} %get-tuple-element.16.grad, ...), custom_call_target="tpu_custom_call" | custom-call | tf_op jit(solution)/shard_map/pallas_call | solution.py:634

commit v4 on v3

--- a/solution.py
+++ b/solution.py
@@ -478,6 +478,7 @@
     weights_pass(0)
     weights_start(1)
     inputs_start(1)
+    inputs_start(2)
     put_inv(0, 0)
     loads[2].wait()
     loads[3].wait()
@@ -490,17 +491,16 @@
     permuted(1, x0.at[1], True)
     share(1)
     weights_pass(1)
-    inputs_start(2)
-    put_inv(2, 1)
-    forward(0, 1, x0.at[1], 2, 2)
+    inputs_wait(2)
+    permuted(2, dy, False)
     e0[0].wait()
     put_entering(0, entering(ey0.at[0]))
     next_layer(x0.at[0], 0, x1.at[0])
     share(2)
+    put_inv(2, 1)
+    forward(0, 1, x0.at[1], 2, 2)
     summarise(2, ey0.at[1])
     e0[1].start()
-    inputs_wait(2)
-    permuted(2, dy, False)
     weights_wait(1)
     assemble(1)
     put_inv(1, 2)
@@ -513,12 +513,12 @@
     put_entering(2, entering(ey0.at[1]))
     next_layer(x0.at[1], 2, x1.at[1])
     share(3)
-    put_inv(2, 3)
     e1.wait()
     put_entering(1, entering(ey1))
     put_entering(4, entering_back(ey1, ey1, 2))
     backward(1, x1.at[0])
     share(4)
+    put_inv(2, 3)
     forward(1, 1, x1.at[1], 2, 2)
     put_rows(3, shared(4))
     through_norm(1, x1.at[0], lambda cols: scan_back(0, cols))
@@ -537,6 +537,7 @@
     last_layer(x1.at[1], 2)
     for d in (2, 1, 3, 0):
         deliver(0, acts_out, 1, d)
+    pass_sums(1)
     put_rows(3, shared(5))
 
     def finish(cols):
@@ -545,7 +546,6 @@
     for d in (2, 1, 3, 0):
         through_norm(0, x0.at[0], finish, mine * xp(d), mine * xp(d) + mine)
         deliver(1, grad_out, -1, d)
-    pass_sums(1)
     pass_sums(0)
     put_sums(1)
     put_sums(0)

time: 91.6 us -> 90.8 us (level); the launches traced: 91.4 us -> 89.4 us
  Pallas kernels: 90.1 us -> 88.1 us
    pallas_call x1, Pallas kernels: 87.8 us -> 85.8 us  [local(): pl.pallas_call(kernel, out_shape=[jax.ShapeDtypeStruct((tokens, chans), B...]
where the time goes in v4:
time: 90.8 us; the launch traced here: 89.4 us
  Pallas kernels  88.1 us (97%)
  between operations  1.29 us (1%)
    pallas_call x1, Pallas kernels, local(): pl.pallas_call(kernel, out_shape=[jax.ShapeDtypeStruct((tokens, chans), B...  85.8 us
    pallas_call x1, Pallas kernels, local(): pl.pallas_call(hand_over, out_shape=[jax.ShapeDtypeStruct((tokens, chans)...  2.23 us

profile of v4, /device:TPU:1, one launch (start us, length us, event | category | flops | bytes accessed | tf_op | source)
XLA Modules:
  0.0 89.4 jit_solution(7576419490064030746)
XLA Ops:
  1.3 85.8 %shard_map.145 = (bf16[128,2048]{1,0:T(8,128)(2,1)}, bf16[128,2048]{1,0:T(8,128)(2,1)}, f32[2,4,16,128]{3,2,1,0:T(8,128)}) custom-call(bf16[128,2048]{1,0:T(8,128)(2,1)} %bitcast.15, bf16[128,2048]{1,0:T(8,128)(2,1)} %bitcast.16, bf16[128,2048]{1,0:T(8,128)(2,1)} %bitcast.17, bf16[2,4,2,8,256]{4,3,2,1,0:T(8,128)(2,1)} %bitcast.18, ...), custom_call_target="tpu_custom_call" | custom-call | tf_op jit(solution)/shard_map/pallas_call | solution.py:578
  87.1 2.2 %shard_map.146 = (bf16[128,2048]{1,0:T(8,128)(2,1)}, bf16[128,2048]{1,0:T(8,128)(2,1)}, f32[2,2048]{1,0:T(2,128)}, f32[2,2048]{1,0:T(2,128)}, f32[2,2048]{1,0:T(2,128)}, /*index=5*/f32[2,2048]{1,0:T(2,128)}) custom-call(bf16[128,2048]{1,0:T(8,128)(2,1)} %get-tuple-element.15.acts, bf16[128,2048]{1,0:T(8,128)(2,1)} %get-tuple-element.16.grad, ...), custom_call_target="tpu_custom_call" | custom-call | tf_op jit(solution)/shard_map/pallas_call | solution.py:634
